TPU v7x, 32 devices: a whole 2x2x4 slice. The times are simulated.
32 devices in a mesh: dp: 8 (over z, core), chan: 4 (over y, x).
Axes of the slice: x: 2, y: 2, z: 4, core: 2. Of those that a mesh axis runs over, the one named last changes fastest.
Arguments:
- feat_in: bfloat16 [512, 32, 1024], P('chan', 'dp'), may hold values from -6 to 6
- rgb_in: float32 [32, 3, 1024], P('dp'), may hold values from -6 to 6
- latent: float32 [32, 512], P('dp'), may hold values from -6 to 6
- noise_first: float32 [32, 4096], P('dp'), may hold values from -6 to 6
- noise_second: float32 [32, 4096], P('dp'), may hold values from -6 to 6
- live_count: int32 [8], P('dp'), may hold values from 1 to 4, 24 in all
- conv_first: bfloat16 [9, 512, 512], P(None, 'chan'), may hold values from -0.09375 to 0.09375
- conv_second: bfloat16 [9, 512, 512], P(None, 'chan'), may hold values from -0.09375 to 0.09375
- style_weight: float32 [3, 512, 512], P(None, None, 'chan'), may hold values from -0.25 to 0.25
- style_bias: float32 [3, 512], P(None, 'chan'), may hold values from 0.5 to 1.5
- rgb_weight: bfloat16 [3, 512], P(None, 'chan'), may hold values from -0.25 to 0.25
- conv_bias: float32 [2, 512], P(None, 'chan'), may hold values from -3 to 3
- rgb_bias: float32 [3], replicated, may hold values from -3 to 3
- noise_gain: float32 [2], replicated, may hold values from 0.2 to 1
- feat_grad: bfloat16 [512, 32, 4096], P('chan', 'dp'), may hold values from -6 to 6
- rgb_grad: float32 [32, 3, 4096], P('dp'), may hold values from -6 to 6
Outputs:
- feat_out: bfloat16 [512, 32, 4096], P('chan', 'dp')
- rgb_out: float32 [32, 3, 4096], P('dp', None, 'chan')
- feat_in_grad: float32 [512, 32, 1024], P('chan', 'dp')
- rgb_in_grad: float32 [32, 3, 1024], P('dp')
- latent_grad: float32 [32, 512], P('dp')
- conv_first_grad: float32 [9, 512, 512], P(None, 'chan')
- conv_second_grad: float32 [9, 512, 512], P(None, 'chan')
- style_weight_grad: float32 [3, 512, 512], P(None, None, 'chan')
- style_bias_grad: float32 [3, 512], P(None, 'chan')
- rgb_weight_grad: float32 [3, 512], P(None, 'chan')
- conv_bias_grad: float32 [2, 512], P(None, 'chan')
- rgb_bias_grad: float32 [3], replicated
- noise_gain_grad: float32 [2], replicated
Inputs may be any that keep to these rules, and one draw needn't show every extreme that they name: Shard s holds images in its first live_count[s] slots of 4; its other slots are empty. The counts add up to 24, and some shard is full.
All inputs are finite; a program needn't handle non-finite values.
Results may differ from a plain program's by a relative error of at most 0.0059.
Values may be sent and summed in bfloat16 or wider, within the bound.
A program may use at most 320 MiB of HBM per device.

v0:
```python
import jax
import jax.numpy as jnp
from jax import lax
from jax.sharding import PartitionSpec as P

SIDE = 64
HALF = 32


precise = lax.Precision.HIGHEST
epsilon = 1e-08
root_two = 1.4142135623730951
phase_taps = (((1, 0),), ((2, 0), (0, 1)))
phase_pairs = ((0, 0), (0, 1), (1, 0), (1, 1))


def leaky_silu(value):
    return root_two * (0.2 * value + 0.8 * jax.nn.silu(value))


def leaky_slope(value):
    sigma = jax.nn.sigmoid(value)
    return root_two * (0.2 + 0.8 * sigma * (1.0 + value * (1.0 - sigma)))


def shifted(field, row_shift, col_shift, width):
    cells = field.shape[-1]
    offset = row_shift * width + col_shift
    if offset > 0:
        result = jnp.concatenate(
            [field[..., offset:], jnp.zeros(field.shape[:-1] + (offset,), field.dtype)], axis=-1
        )
    elif offset < 0:
        result = jnp.concatenate(
            [jnp.zeros(field.shape[:-1] + (-offset,), field.dtype), field[..., : cells + offset]],
            axis=-1,
        )
    else:
        result = field
    if col_shift != 0:
        column = jnp.arange(cells) % width
        inside = (column + col_shift >= 0) & (column + col_shift < width)
        result = jnp.where(inside, result, jnp.zeros((), field.dtype))
    return result


def upsample_matrix(half_side):
    rows_out = jnp.arange(2 * half_side)[:, None]
    cols_in = jnp.arange(half_side)[None, :]
    centre = rows_out // 2
    beside = centre - 1 + 2 * (rows_out % 2)
    return (
        jnp.where(cols_in == centre, 0.75, 0.0) + jnp.where(cols_in == beside, 0.25, 0.0)
    ).astype(jnp.float32)


def alternate(phases, half_side):
    stacked = jnp.stack(phases)
    out_rows, batch_count = (stacked.shape[1], stacked.shape[2])
    blocked = stacked.reshape(2, 2, out_rows, batch_count, half_side, half_side)
    return blocked.transpose(2, 3, 4, 0, 5, 1).reshape(
        out_rows, batch_count, 4 * half_side * half_side
    )


def split_phases(field, half_side):
    out_rows, batch_count = (field.shape[0], field.shape[1])
    blocked = field.reshape(out_rows, batch_count, half_side, 2, half_side, 2)
    return [
        blocked[:, :, :, row_phase, :, col_phase].reshape(
            out_rows, batch_count, half_side * half_side
        )
        for row_phase, col_phase in phase_pairs
    ]


def up_conv(inputs, weight, half_side):
    shifted_inputs = {}
    for row_shift in (0, 1):
        for col_shift in (0, 1):
            shifted_inputs[row_shift, col_shift] = shifted(inputs, row_shift, col_shift, half_side)
    phases = []
    for row_phase, col_phase in phase_pairs:
        summed = None
        for row_tap, row_shift in phase_taps[row_phase]:
            for col_tap, col_shift in phase_taps[col_phase]:
                product = jnp.einsum(
                    "oc,cbp->obp",
                    weight[row_tap * 3 + col_tap],
                    shifted_inputs[row_shift, col_shift],
                    preferred_element_type=jnp.float32,
                )
                summed = product if summed is None else summed + product
        phases.append(summed)
    return alternate(phases, half_side)


def phase_grads(grad_field, half_side):
    grad_phases = split_phases(grad_field, half_side)
    shifted_grads = [None] * 9
    for phase_index in range(4):
        row_phase, col_phase = phase_pairs[phase_index]
        for row_tap, row_shift in phase_taps[row_phase]:
            for col_tap, col_shift in phase_taps[col_phase]:
                shifted_grads[row_tap * 3 + col_tap] = shifted(
                    grad_phases[phase_index], -row_shift, -col_shift, half_side
                )
    return shifted_grads


def flat_conv(inputs, weight, width):
    summed = None
    for tap_index in range(9):
        product = jnp.einsum(
            "oc,cbp->obp", weight[tap_index], inputs, preferred_element_type=jnp.float32
        )
        product = shifted(product, tap_index // 3 - 1, tap_index % 3 - 1, width)
        summed = product if summed is None else summed + product
    return summed


def body(
    feat_in,
    rgb_in,
    latent,
    noise_first,
    noise_second,
    live_count,
    conv_first,
    conv_second,
    style_weight,
    style_bias,
    rgb_weight,
    conv_bias,
    rgb_bias,
    noise_gain,
    feat_grad,
    rgb_grad,
):
    local_ch, images, half_pix = feat_in.shape
    pixels = feat_grad.shape[2]
    half_side = HALF
    full_side = SIDE
    chan_rank = lax.axis_index("chan")
    live_mask = (jnp.arange(images) < live_count[0]).astype(jnp.float32)
    styles = (
        jnp.einsum("bw,jwc->jbc", latent, style_weight, precision=precise) + style_bias[:, None, :]
    )
    first_all, second_all = (
        lax.all_gather(styles[0], "chan", axis=1, tiled=True),
        lax.all_gather(styles[1], "chan", axis=1, tiled=True),
    )
    weight_one = conv_first.astype(jnp.float32)
    weight_two = conv_second.astype(jnp.float32)
    squares_one = jnp.sum(weight_one * weight_one, axis=0)
    squares_two = jnp.sum(weight_two * weight_two, axis=0)
    demod_one = lax.rsqrt(
        jnp.dot(first_all * first_all, squares_one.T, precision=precise) + epsilon
    )
    demod_two = lax.rsqrt(
        jnp.dot(second_all * second_all, squares_two.T, precision=precise) + epsilon
    )
    scaled_one = (feat_in.astype(jnp.float32) * styles[0].T[:, :, None]).astype(jnp.bfloat16)
    gathered_one = lax.all_gather(scaled_one, "chan", axis=0, tiled=True)
    raised = up_conv(gathered_one, conv_first, half_side)
    pre_one = (
        raised * demod_one.T[:, :, None]
        + noise_gain[0] * noise_first[None, :, :]
        + conv_bias[0][:, None, None]
    )
    act_one = leaky_silu(pre_one)
    scaled_two = (act_one * styles[1].T[:, :, None]).astype(jnp.bfloat16)
    gathered_two = lax.all_gather(scaled_two, "chan", axis=0, tiled=True)
    convolved = flat_conv(gathered_two, conv_second, full_side)
    pre_two = (
        convolved * demod_two.T[:, :, None]
        + noise_gain[1] * noise_second[None, :, :]
        + conv_bias[1][:, None, None]
    )
    act_two = leaky_silu(pre_two)
    feat_out = (act_two * live_mask[None, :, None]).astype(jnp.bfloat16)
    scaled_rgb = (act_two * styles[2].T[:, :, None]).astype(jnp.bfloat16)
    color_part = jnp.einsum(
        "ko,obp->bkp", rgb_weight, scaled_rgb, preferred_element_type=jnp.float32
    )
    color = lax.psum_scatter(color_part, "chan", scatter_dimension=2, tiled=True)
    shard_pix = color.shape[2]
    lift_matrix = upsample_matrix(half_side)
    skip_up = jnp.einsum(
        "up,bkpq,vq->bkuv",
        lift_matrix,
        rgb_in.reshape(images, 3, half_side, half_side),
        lift_matrix,
        precision=precise,
    ).reshape(images, 3, pixels)
    skip_mine = lax.dynamic_slice_in_dim(skip_up, chan_rank * shard_pix, shard_pix, 2)
    rgb_out = (color + rgb_bias[None, :, None] + skip_mine) * live_mask[:, None, None]
    rgb_cot = rgb_grad * live_mask[:, None, None]
    color_cot = rgb_cot.astype(jnp.bfloat16)
    rgb_in_grad = jnp.einsum(
        "up,bkuv,vq->bkpq",
        lift_matrix,
        rgb_cot.reshape(images, 3, full_side, full_side),
        lift_matrix,
        precision=precise,
    ).reshape(images, 3, half_pix)
    rgb_bias_part = jnp.sum(rgb_cot, axis=(0, 2))
    rgb_weight_part = jnp.einsum(
        "bkp,obp->ko", color_cot, scaled_rgb, preferred_element_type=jnp.float32
    )
    back_rgb = jnp.einsum("ko,bkp->obp", rgb_weight, color_cot, preferred_element_type=jnp.float32)
    style_rgb_grad = jnp.sum(back_rgb * act_two, axis=2).T
    grad_pre_two = (
        feat_grad.astype(jnp.float32) * live_mask[None, :, None]
        + back_rgb * styles[2].T[:, :, None]
    ) * leaky_slope(pre_two)
    cot_two = (grad_pre_two * demod_two.T[:, :, None]).astype(jnp.bfloat16)
    inner_two = (
        -0.5 * demod_two * demod_two * demod_two * jnp.sum(grad_pre_two * convolved, axis=2).T
    )
    taps_two = jnp.stack(
        [
            shifted(cot_two, 1 - tap_index // 3, 1 - tap_index % 3, full_side)
            for tap_index in range(9)
        ]
    )
    squares_two_grad = jnp.dot(inner_two.T, second_all * second_all, precision=precise)
    conv_two_grad = (
        jnp.einsum("tobp,cbp->toc", taps_two, gathered_two, preferred_element_type=jnp.float32)
        + 2.0 * weight_two * squares_two_grad[None]
    )
    style_two_demod = 2.0 * second_all * jnp.dot(inner_two, squares_two, precision=precise)
    columns = conv_second
    back_two = lax.psum_scatter(
        jnp.einsum("toc,tobp->cbp", columns, taps_two, preferred_element_type=jnp.float32),
        "chan",
        scatter_dimension=0,
        tiled=True,
    )
    style_two_conv = jnp.sum(back_two * act_one, axis=2).T
    grad_pre_one = back_two * styles[1].T[:, :, None] * leaky_slope(pre_one)
    cot_one = (grad_pre_one * demod_one.T[:, :, None]).astype(jnp.bfloat16)
    inner_one = -0.5 * demod_one * demod_one * demod_one * jnp.sum(grad_pre_one * raised, axis=2).T
    taps_one = jnp.stack(phase_grads(cot_one, half_side))
    squares_one_grad = jnp.dot(inner_one.T, first_all * first_all, precision=precise)
    conv_one_grad = (
        jnp.einsum("tobp,cbp->toc", taps_one, gathered_one, preferred_element_type=jnp.float32)
        + 2.0 * weight_one * squares_one_grad[None]
    )
    style_one_demod = 2.0 * first_all * jnp.dot(inner_one, squares_one, precision=precise)
    columns = conv_first
    back_one = lax.psum_scatter(
        jnp.einsum("toc,tobp->cbp", columns, taps_one, preferred_element_type=jnp.float32),
        "chan",
        scatter_dimension=0,
        tiled=True,
    )
    feat_in_grad = back_one * styles[0].T[:, :, None]
    style_one_conv = jnp.sum(back_one * feat_in.astype(jnp.float32), axis=2).T
    demod_one_sum, demod_two_sum = (
        lax.psum_scatter(style_one_demod, "chan", scatter_dimension=1, tiled=True),
        lax.psum_scatter(style_two_demod, "chan", scatter_dimension=1, tiled=True),
    )
    style_grads = jnp.stack(
        [style_one_conv + demod_one_sum, style_two_conv + demod_two_sum, style_rgb_grad]
    )
    latent_part = jnp.einsum("jbc,jwc->bw", style_grads, style_weight, precision=precise)
    gain_part = jnp.stack(
        [
            jnp.sum(grad_pre_one * noise_first[None, :, :]),
            jnp.sum(grad_pre_two * noise_second[None, :, :]),
        ]
    )
    latent_grad, gain_chan = lax.psum((latent_part, gain_part), "chan")
    style_weight_part = jnp.einsum("bw,jbc->jwc", latent, style_grads, precision=precise)
    style_bias_part = jnp.sum(style_grads, axis=1)
    conv_bias_part = jnp.stack(
        [jnp.sum(grad_pre_one, axis=(1, 2)), jnp.sum(grad_pre_two, axis=(1, 2))]
    )
    totals = lax.psum(
        (
            conv_one_grad,
            conv_two_grad,
            style_weight_part,
            style_bias_part,
            rgb_weight_part,
            conv_bias_part,
            rgb_bias_part,
            gain_chan,
        ),
        "dp",
    )
    return (feat_out, rgb_out, feat_in_grad, rgb_in_grad, latent_grad) + tuple(totals)


def solution(mesh):
    return jax.shard_map(
        body,
        mesh=mesh,
        in_specs=(
            P("chan", "dp", None),
            P("dp", None, None),
            P("dp", None),
            P("dp", None),
            P("dp", None),
            P("dp"),
            P(None, "chan", None),
            P(None, "chan", None),
            P(None, None, "chan"),
            P(None, "chan"),
            P(None, "chan"),
            P(None, "chan"),
            P(),
            P(),
            P("chan", "dp", None),
            P("dp", None, None),
        ),
        out_specs=(
            P("chan", "dp", None),
            P("dp", None, "chan"),
            P("chan", "dp", None),
            P("dp", None, None),
            P("dp", None),
            P(None, "chan", None),
            P(None, "chan", None),
            P(None, None, "chan"),
            P(None, "chan"),
            P(None, "chan"),
            P(None, "chan"),
            P(),
            P(),
        ),
        check_vma=False,
    )
```

profile of v0, /device:TPU:0, one launch (start us, length us, event | category | flops | bytes accessed | tf_op | source)
XLA Modules:
  0.0 1091.2 jit_solution(2586246436795149009)
XLA Ops:
  13.4 9.5 all-gather
  29.1 39.7 %all-gather.5.cloned.1.call-done = bf16[512,4,1024]{0,2,1:T(8,128)(2,1)} async-done(((bf16[128,4,1024]{0,2,1:T(8,128)(2,1)}), bf16[512,4,1024]{0,2,1:T(8,128)(2,1)}) %all-gather.5.cloned.1.call-update) | async-done | bytes 4194320 | tf_op jit(solution)/shard_map/all_gather | solution.py:164
  86.1 7.5 copy.79
  105.1 8.2 copy.84
  113.3 8.0 all-gather.1
  128.3 132.0 %all-gather.7.cloned.1.call-done = bf16[512,4,4096]{0,2,1:T(8,128)(2,1)} async-done(((bf16[128,4,4096]{0,2,1:T(8,128)(2,1)}), bf16[512,4,4096]{0,2,1:T(8,128)(2,1)}) %all-gather.7.cloned.1.call-update) | async-done | bytes 16777232 | tf_op jit(solution)/shard_map/all_gather | solution.py:173
  260.3 13.8 %convolution_bitcast_fusion.4 = f32[128,4,4096]{0,2,1:T(8,128)} fusion(bf16[512,4,4096]{0,2,1:T(8,128)(2,1)} %all-gather.7.cloned.1.call-done, bf16[9,128,512]{2,1,0:T(8,128)(2,1)S(1)} %copy-done.7), kind=kOutput, calls=%fused_computation.34 | convolution fusion | flops 2147483648 | bytes 25296896 | tf_op jit(solution)/shard_map/oc,cbp->obp/dot_general | solution.py:114
  274.1 7.4 slice.226
  329.8 7.1 slice.223
  371.3 32.3 %multiply_reduce_fusion = (f32[]{:T(128)}, f32[128]{0:T(128)}, f32[128,4]{0,1:T(4,128)S(1)}, f32[128,4,4096]{0,2,1:T(8,128)}, f32[128,4]{0,1:T(4,128)}, /*index=5*/f32[128,4,4096]{0,2,1:T(8,128)}) fusion(f32[4,4096]{1,0:T(4,128)S(1)} %copy-done.31, f32[128]{0:T(128)S(1)} %get-tuple-element.99, f32[4,4096]{1,0:T(4,128)S(1)} %broadcast_multiply_fusion.2, ...), kind=kOutput, calls=%fused_computation.14 | convolution fusion | flops 2239757312 | bytes 112735744 | tf_op jit(solution)/shard_map/oc,cbp->obp/dot_general | solution.py:114
  442.0 30.6 %convolution_bitcast_fusion = f32[512,4,4096]{0,2,1:T(8,128)} fusion(bf16[9,128,4,4096]{1,3,2,0:T(8,128)(2,1)} %bitcast_dynamic-update-slice_fusion, bf16[9,128,512]{2,1,0:T(8,128)(2,1)S(1)} %copy-done.8), kind=kOutput, calls=%fused_computation.2 | convolution fusion | flops 19327352832 | bytes 72482816 | tf_op jit(solution)/shard_map/toc,tobp->cbp/dot_general | solution.py:235
  474.7 286.7 %reduce-scatter.12.cloned.1.call-done = f32[128,4,4096]{0,2,1:T(8,128)} async-done(((f32[512,4,4096]{0,2,1:T(8,128)}), f32[128,4,4096]{0,2,1:T(8,128)}) %reduce-scatter.12.cloned.1.call-update) | async-done | bytes 8388624 | tf_op jit(solution)/shard_map/reduce_scatter | solution.py:234
  761.5 12.0 %multiply_reduce_fusion.1 = (f32[]{:T(128)}, f32[128]{0:T(128)}, f32[128,4]{0,1:T(4,128)S(1)}, f32[128,4]{0,1:T(4,128)}, f32[128,4,4096]{0,2,1:T(8,128)S(1)}) fusion(f32[4,4096]{1,0:T(4,128)S(1)} %copy-done.22, f32[128,4,4096]{0,2,1:T(8,128)} %bitcast.362, f32[128,4,4096]{0,2,1:T(8,128)} %reduce-scatter.12.cloned.1.call-done, f32[128]{0:T(128)S(1)} %copy-done.49, ...), kind=kLoop, calls=%fused_computation.15 | loop fusion | flops 56621952 | bytes 25306116 | tf_op jit(solution)/shard_map/reduce_sum | solution.py:270
  774.1 8.9 fusion.183
  796.6 10.1 convolution_bitcast_fusion.10
  820.7 7.7 reshape.178
  830.3 29.0 %fusion.22 = f32[9,128,512]{2,1,0:T(8,128)} fusion(bf16[9,128,512]{2,1,0:T(8,128)(2,1)S(1)} %copy-done.9, bf16[9,128,4,4096]{1,3,2,0:T(8,128)(2,1)} %bitcast_dynamic-update-slice_fusion, bf16[512,4,4096]{0,2,1:T(8,128)(2,1)} %all-gather.7.cloned.1.call-done, f32[128,512]{1,0:T(8,128)} %convolution_multiply_fusion), kind=kOutput, calls=%fused_computation.70 | convolution fusion | flops 19329122304 | bytes 58327040 | tf_op jit(solution)/shard_map/tobp,cbp->toc/dot_general | solution.py:229
  861.4 11.4 %fusion.20 = f32[9,128,512]{2,1,0:T(8,128)} fusion(bf16[9,128,512]{2,1,0:T(8,128)(2,1)S(1)} %copy-done.11, bf16[9,128,4,1024]{1,3,0,2:T(8,128)(2,1)} %constant_dynamic-update-slice_fusion, bf16[512,4,1024]{0,2,1:T(8,128)(2,1)} %all-gather.5.cloned.1.call-done, f32[128,512]{1,0:T(8,128)S(1)} %convolution_multiply_fusion.1), kind=kOutput, calls=%fused_computation.68 | convolution fusion | flops 4833607680 | bytes 17432576 | tf_op jit(solution)/shard_map/tobp,cbp->toc/dot_general | solution.py:247
  873.7 36.7 %reduce-scatter.14.cloned.1.call-done = f32[128,4,1024]{0,2,1:T(8,128)} async-done(((f32[512,4,1024]{0,2,1:T(8,128)}), f32[128,4,1024]{0,2,1:T(8,128)}) %reduce-scatter.14.cloned.1.call-update) | async-done | bytes 2097168 | tf_op jit(solution)/shard_map/reduce_scatter | solution.py:252
  923.0 7.9 copy.104
  935.1 14.1 %reduce-scatter.16.cloned.1.call-done = f32[1024,12]{1,0:T(8,128)} async-done(((f32[4096,12]{1,0:T(8,128)}), f32[1024,12]{1,0:T(8,128)}) %reduce-scatter.16.cloned.1.call-update) | async-done | bytes 49168
  958.9 9.8 all-reduce.26
  968.8 16.7 %all-reduce.24 = (f32[3,128]{1,0:T(4,128)}, f32[3,128]{1,0:T(4,128)}, f32[2,128]{1,0:T(2,128)}, f32[3]{0:T(128)}, f32[2]{0:T(128)}) all-reduce(f32[3,128]{1,0:T(4,128)S(1)} %fusion.180, f32[3,128]{1,0:T(4,128)S(1)} %fusion.39, f32[2,128]{1,0:T(2,128)S(1)} %pad_maximum_fusion.2, ...), channel_id=1, replica_groups=mesh['dp'=8,'chan'=4] {'dp'}, use_global_device_ids=true, to_apply=%region_17.18 | all-reduce | flops 1029 | bytes 8232 | tf_op jit(solution)/shard_map/psum | solution.py:280
  985.5 89.6 %all-reduce.29.cloned.1.call-done = (f32[9,128,512]{2,1,0:T(8,128)}, f32[9,128,512]{2,1,0:T(8,128)}, f32[3,512,128]{1,2,0:T(8,128)}) async-done(((f32[9,128,512]{2,1,0:T(8,128)}, f32[9,128,512]{2,1,0:T(8,128)}, f32[3,512,128]{1,2,0:T(8,128)}), (f32[9,128,512]{2,1,0:T(8,128)}, f32[9,128,512]{2,1,0:T(8,128)}, f32[3,512,128]{1,2,0:T(8,128)})) %all-reduce.29.cloned.1.call-update) | async-done | bytes 5505040 | tf_op jit(solution)/shard_map/psum | solution.py:280
  (262 shorter events, 238.4 us)
Async XLA Ops:
  7.2 65.0 %copy-start.10 = (bf16[9,128,512]{2,1,0:T(8,128)(2,1)S(1)}, bf16[9,128,512]{2,1,0:T(8,128)(2,1)}, u32[]{:S(2)}) copy-start(bf16[9,128,512]{2,1,0:T(8,128)(2,1)} %param.22) | copy-start | bytes 3538948
  7.2 61.6 %all-gather.5.cloned.1.call-start = ((), (), s32[]{:S(2)}) async-start(), calls=%async_computation.5 | async-start | bytes 5242880 | tf_op jit(solution)/shard_map/all_gather | solution.py:164
  12.1 61.4 %copy-start.5 = (bf16[128,4,1024]{0,2,1:T(8,128)(2,1)}, bf16[128,4,1024]{0,2,1:T(8,128)(2,1)S(1)}, u32[]{:S(2)}) copy-start(bf16[128,4,1024]{0,2,1:T(8,128)(2,1)S(1)} %copy.78) | copy-start | bytes 3145732
  13.4 246.9 %all-gather.7.cloned.1.call-start = ((), (), s32[]{:S(2)}) async-start(), calls=%async_computation.6 | async-start | bytes 20971520 | tf_op jit(solution)/shard_map/all_gather | solution.py:173
  26.7 66.9 %copy-start.48 = (f32[128]{0:T(128)}, f32[128]{0:T(128)S(1)}, u32[]{:S(2)}) copy-start(f32[128]{0:T(128)S(1)} %get-tuple-element.98) | copy-start | bytes 1540
  27.5 66.1 %copy-start.28 = (f32[4,128]{1,0:T(4,128)}, f32[4,128]{1,0:T(4,128)S(1)}, u32[]{:S(2)}) copy-start(f32[4,128]{1,0:T(4,128)S(1)} %fusion.41) | copy-start | bytes 6148
  29.1 64.5 %copy-start.20 = (f32[4,4096]{1,0:T(4,128)}, f32[4,4096]{1,0:T(4,128)S(1)}, u32[]{:S(2)}) copy-start(f32[4,4096]{1,0:T(4,128)S(1)} %broadcast_multiply_fusion.3) | copy-start | bytes 196612
  102.8 658.6 %reduce-scatter.12.cloned.1.call-start = ((), (), s32[]{:S(2)}) async-start(), calls=%async_computation.7 | async-start | bytes 41943040 | tf_op jit(solution)/shard_map/reduce_scatter | solution.py:234
  103.6 267.7 %copy-start.52 = (f32[4]{0:T(128)}, f32[4]{0:T(128)S(1)}, u32[]{:S(2)}) copy-start(f32[4]{0:T(128)S(1)} %compare_convert_fusion) | copy-start | bytes 52
  122.6 350.1 %copy-start.32 = (f32[4,128]{1,0:T(4,128)}, f32[4,128]{1,0:T(4,128)S(1)}, u32[]{:S(2)}) copy-start(f32[4,128]{1,0:T(4,128)S(1)} %fusion.40) | copy-start | bytes 6148
  403.6 69.1 %copy-start.42 = (f32[128,4]{0,1:T(4,128)}, f32[128,4]{0,1:T(4,128)S(1)}, u32[]{:S(2)}) copy-start(f32[128,4]{0,1:T(4,128)S(1)} %get-tuple-element.58) | copy-start | bytes 6148
  472.6 288.9 %copy-start.21 = (f32[4,4096]{1,0:T(4,128)S(1)}, f32[4,4096]{1,0:T(4,128)}, u32[]{:S(2)}) copy-start(f32[4,4096]{1,0:T(4,128)} %copy-done.20) | copy-start | bytes 196612
  472.6 288.9 %copy-start.22 = (f32[4,4096]{1,0:T(4,128)S(1)}, f32[4,4096]{1,0:T(4,128)}, u32[]{:S(2)}) copy-start(f32[4,4096]{1,0:T(4,128)} %param.19) | copy-start | bytes 196612
  472.6 288.8 %copy-start.29 = (f32[4,128]{1,0:T(4,128)S(1)}, f32[4,128]{1,0:T(4,128)}, u32[]{:S(2)}) copy-start(f32[4,128]{1,0:T(4,128)} %copy-done.28) | copy-start | bytes 6148
  472.6 288.8 %copy-start.47 = (f32[128,4]{0,1:T(4,128)S(1)}, f32[128,4]{0,1:T(4,128)}, u32[]{:S(2)}) copy-start(f32[128,4]{0,1:T(4,128)} %get-tuple-element.91) | copy-start | bytes 6148
  472.6 288.8 %copy-start.49 = (f32[128]{0:T(128)S(1)}, f32[128]{0:T(128)}, u32[]{:S(2)}) copy-start(f32[128]{0:T(128)} %copy-done.48) | copy-start | bytes 1540
  472.7 386.6 %reduce-scatter.20.cloned.1.call-start = ((), (), s32[]{:S(2)}) async-start(), calls=%async_computation.11 | async-start | bytes 327680
  474.7 398.1 %reduce-scatter.18.cloned.1.call-start = ((), (), s32[]{:S(2)}) async-start(), calls=%async_computation.10 | async-start | bytes 327680
  796.5 113.9 %reduce-scatter.14.cloned.1.call-start = ((), (), s32[]{:S(2)}) async-start(), calls=%async_computation.8 | async-start | bytes 10485760 | tf_op jit(solution)/shard_map/reduce_scatter | solution.py:252
  806.7 142.4 %reduce-scatter.16.cloned.1.call-start = ((), (), s32[]{:S(2)}) async-start(), calls=%async_computation.9 | async-start | bytes 2621440
  830.3 244.9 %all-reduce.29.cloned.1.call-start = ((), (), s32[]{:S(2)}) async-start(), calls=%async_computation.12 | async-start | bytes 11010048 | tf_op jit(solution)/shard_map/psum | solution.py:280
  861.4 49.0 %copy-start.37 = (f32[128,4]{0,1:T(4,128)S(1)}, f32[128,4]{0,1:T(4,128)}, u32[]{:S(2)}) copy-start(f32[128,4]{0,1:T(4,128)} %copy-done.36) | copy-start | bytes 6148
  861.4 52.3 %copy-start.34 = (f32[4,512]{1,0:T(4,128)S(1)}, f32[4,512]{1,0:T(4,128)}, u32[]{:S(2)}) copy-start(f32[4,512]{1,0:T(4,128)} %param.18) | copy-start | bytes 24580
  861.4 52.3 %copy-start.35 = (f32[128,4]{0,1:T(4,128)S(1)}, f32[128,4]{0,1:T(4,128)}, u32[]{:S(2)}) copy-start(f32[128,4]{0,1:T(4,128)} %get-tuple-element.75) | copy-start | bytes 6148
  (48 other events, 635.8 us)
Sparse Core Ops, SparseCore 0:
  13.5 55.2 all-gather.4
  103.0 157.3 all-gather.6
  472.8 288.6 reduce-scatter.11
  764.9 24.0 reduce-scatter.19
  796.7 24.0 reduce-scatter.17
  824.0 86.3 reduce-scatter.13
  913.9 35.1 reduce-scatter.15
  952.5 122.5 all-reduce.28
where the time goes:
time: 1100 us; the launch traced here: 1090 us
  waiting for transfers between devices  599 us (54%)
  matrix products  209 us (19%)
  local copies, waits for them, and re-layouts  154 us (14%)
  other arithmetic  68.3 us (6%)
  blocking collectives  44.1 us (4%)
  between operations  16.1 us (1%)
    reduce_scatter x1, waiting for transfers between devices, body(): lax.psum_scatter(jnp.einsum('toc,tobp->cbp', columns, taps_two, preferred...  287 us
    all_gather x1, waiting for transfers between devices, body(): gathered_two = lax.all_gather(scaled_two, 'chan', axis=0, tiled=True)  132 us
    dot_general x9, matrix products, flat_conv(): jnp.einsum('oc,cbp->obp', weight[tap_index], inputs, preferred_element_ty...  93.3 us
    psum x1, waiting for transfers between devices, body(): lax.psum((conv_one_grad, conv_two_grad, style_weight_part, style_bias_par...  89.6 us
    unnamed x153, local copies, waits for them, and re-layouts  69.1 us
    all_gather x1, waiting for transfers between devices, body(): gathered_one = lax.all_gather(scaled_one, 'chan', axis=0, tiled=True)  39.7 us
    reduce_scatter x1, waiting for transfers between devices, body(): lax.psum_scatter(jnp.einsum('toc,tobp->cbp', columns, taps_one, preferred...  36.7 us
    slice x7, local copies, waits for them, and re-layouts, shifted(): field[..., offset:]  33.2 us
  transfers between devices with their start and end apart: 8, of which 6 were waited for; matrix products, arithmetic and copies ran while one was open for 15% of the time, Pallas kernels for 0%

commit v1 on v0

--- a/solution.py
+++ b/solution.py
@@ -1,6 +1,10 @@
+import functools
+
 import jax
 import jax.numpy as jnp
 from jax import lax
+from jax.experimental import pallas as pl
+from jax.experimental.pallas import tpu as pltpu
 from jax.sharding import PartitionSpec as P
 
 SIDE = 64
@@ -293,9 +297,686 @@
     return (feat_out, rgb_out, feat_in_grad, rgb_in_grad, latent_grad) + tuple(totals)
 
 
+BF = jnp.bfloat16
+F32 = jnp.float32
+TILE = 256
+ROWS = 64
+ANY = pl.BlockSpec(memory_space=pl.ANY)
+SMEM = pl.BlockSpec(memory_space=pltpu.SMEM)
+LIMIT = 56 * 1024 * 1024
+
+
+def whole(shape):
+    return pl.BlockSpec(shape, lambda j: (0,) * len(shape))
+
+
+def dot(a, b):
+    return jnp.dot(a, b, preferred_element_type=F32)
+
+
+def dot_nt(a, b):
+    return lax.dot_general(a, b, (((1,), (1,)), ((), ())), preferred_element_type=F32)
+
+
+def wide(column):
+    return jnp.concatenate([column] * (TILE // 128), axis=1)
+
+
+def move(field, row_shift, col_shift):
+    offset = row_shift * HALF + col_shift
+    if offset == 0:
+        return field
+    cells = field.shape[1]
+    lane = lax.broadcasted_iota(jnp.int32, field.shape, 1)
+    row, col = lane // HALF, lane % HALF
+    inside = (row + row_shift >= 0) & (row + row_shift < HALF)
+    inside = inside & (col + col_shift >= 0) & (col + col_shift < HALF)
+    rolled = pltpu.roll(field.astype(F32), (-offset) % cells, 1)
+    return jnp.where(inside, rolled, 0.0).astype(field.dtype)
+
+
+def near(parity, step):
+    other = (parity + step) % 2
+    return other, (parity + step - other) // 2
+
+
+def copy_index(phase, row_step, col_step):
+    a, r = near(phase // 2, row_step)
+    b, q = near(phase % 2, col_step)
+    return ((a * 2 + b) * 2 + abs(r)) * 2 + abs(q)
+
+
+def make_copies(source, copies):
+    chunk = 32
+
+    @pl.loop(0, source.shape[1] // chunk)
+    def _(i):
+        rows = pl.ds(pl.multiple_of(i * chunk, chunk), chunk)
+        for phase in range(4):
+            field = source[phase, rows, :]
+            row_sign = 1 if phase // 2 == 0 else -1
+            col_sign = 1 if phase % 2 == 0 else -1
+            for r in (0, 1):
+                for q in (0, 1):
+                    copies[(phase * 2 + r) * 2 + q, rows, :] = move(
+                        field, row_sign * r, col_sign * q
+                    )
+
+
+def weight_copies(me, core, own, others, swapped, full, sem):
+    result = [(own, pl.ds(pl.multiple_of(me * 128, 128), 128))]
+    for k in (1, 2, 3):
+        base = jnp.bitwise_xor(me, k) * 128
+        result.append((others[k - 1], pl.ds(pl.multiple_of(base + core * 64, 64), 64)))
+        result.append((swapped[k - 1], pl.ds(pl.multiple_of(base + (1 - core) * 64, 64), 64)))
+    return [
+        pltpu.make_async_copy(part, full.at[:, rows, :], sem.at[i])
+        for i, (part, rows) in enumerate(result)
+    ]
+
+
+def demodulate(full, square_row, demod):
+    chunk = 32
+
+    @pl.loop(0, full.shape[1] // chunk)
+    def _(i):
+        rows = pl.ds(pl.multiple_of(i * chunk, chunk), chunk)
+        total = None
+        for t in range(9):
+            value = full[t, rows, :].astype(F32)
+            total = value * value if total is None else total + value * value
+        total = jnp.sum(total * square_row, axis=1, keepdims=True)
+        demod[rows, :] = jnp.broadcast_to(lax.rsqrt(total + epsilon), (chunk, 128))
+
+
+def up_kernel(ids, gains, x0, x1, x2, x3, own, g1, g2, g3, s1, s2, s3, cols, rows_ref, noise,
+              raised, scaled_two, full, scaled_one, demod, copies, sem):
+    j = pl.program_id(0)
+    me, core = ids[0], ids[1]
+
+    @pl.when(j == 0)
+    def _():
+        moves = weight_copies(me, core, own, (g1, g2, g3), (s1, s2, s3), full, sem)
+        for item in moves:
+            item.start()
+        for k, part in enumerate((x0, x1, x2, x3)):
+            base = jnp.bitwise_xor(me, k) * 128
+
+            @pl.loop(0, 128 // 32)
+            def _(i):
+                rows = pl.ds(pl.multiple_of(base + i * 32, 32), 32)
+                here = pl.ds(pl.multiple_of(i * 32, 32), 32)
+                style = jnp.concatenate([cols[0, rows, :]] * 8, axis=1)
+                value = (part[here, :].astype(F32) * style).astype(BF)
+                scaled_one[rows, :] = value
+                for r in (0, 1):
+                    for q in (0, 1):
+                        copies[2 * r + q, rows, :] = move(value, r, q)
+
+        for item in moves:
+            item.wait()
+        demodulate(full, rows_ref[0:1, :], demod)
+
+    here = pl.ds(pl.multiple_of(j * TILE, TILE), TILE)
+    for phase, (row_phase, col_phase) in enumerate(phase_pairs):
+        total = None
+        for k, r in phase_taps[row_phase]:
+            for l, q in phase_taps[col_phase]:
+                term = dot(full[3 * k + l], copies[2 * r + q, :, here])
+                total = term if total is None else total + term
+        raised[phase] = total
+        noise_row = gains[0] * noise[phase : phase + 1, here]
+
+        @pl.loop(0, raised.shape[1] // ROWS)
+        def _(i):
+            rows = pl.ds(pl.multiple_of(i * ROWS, ROWS), ROWS)
+            pre = raised[phase, rows, :] * wide(demod[rows, :]) + noise_row + wide(cols[3, rows, :])
+            act = leaky_silu(pre)
+            scaled_two[phase, rows, :] = (act * wide(cols[1, rows, :])).astype(BF)
+
+
+def conv_kernel(ids, gains, scaled_two, own, g1, g2, g3, s1, s2, s3, cols, rows_ref, noise, order, rgb_rows,
+                convolved, f0, f1, f2, f3, color, full, demod, copies, ordered, for_rgb, sem):
+    j = pl.program_id(0)
+    me, core = ids[0], ids[1]
+
+    @pl.when(j == 0)
+    def _():
+        moves = weight_copies(me, core, own, (g1, g2, g3), (s1, s2, s3), full, sem)
+        for item in moves:
+            item.start()
+        make_copies(scaled_two, copies)
+        for item in moves:
+            item.wait()
+        demodulate(full, rows_ref[1:2, :], demod)
+
+    here = pl.ds(pl.multiple_of(j * TILE, TILE), TILE)
+    live = gains[2]
+    for phase in range(4):
+        total = None
+        for t in range(9):
+            term = dot(full[t], copies[copy_index(phase, t // 3 - 1, t % 3 - 1), :, here])
+            total = term if total is None else total + term
+        convolved[phase] = total
+        noise_row = gains[1] * noise[phase : phase + 1, here]
+
+        @pl.loop(0, convolved.shape[1] // ROWS)
+        def _(i):
+            rows = pl.ds(pl.multiple_of(i * ROWS, ROWS), ROWS)
+            pre = convolved[phase, rows, :] * wide(demod[rows, :]) + noise_row + wide(cols[4, rows, :])
+            act = leaky_silu(pre)
+            out = (act * live).astype(BF)
+            for half in range(TILE // 128):
+                ordered[half, rows, phase * 128 : (phase + 1) * 128] = out[:, half * 128 : (half + 1) * 128]
+            for_rgb[rows, :] = (act * wide(cols[2, rows, :])).astype(BF)
+
+        color[phase] = dot(rgb_rows[...], for_rgb[...])
+    for half in range(TILE // 128):
+        for k, out in enumerate((f0, f1, f2, f3)):
+            rows = pl.ds(pl.multiple_of(jnp.bitwise_xor(me, k) * 128, 128), 128)
+            out[:, half * 512 : (half + 1) * 512] = dot(ordered[half, rows, :], order[...]).astype(BF)
+
+
+def cot_kernel(ids, gains, convolved, d0, d1, d2, d3, cols, demod, noise, order, color_cot, rgb_cols,
+               cot_two, sums, rgb_grad, inner, fields, for_rgb):
+    j = pl.program_id(0)
+    me = ids[0]
+    live = gains[2]
+
+    @pl.when(j == 0)
+    def _():
+        sums[...] = jnp.zeros_like(sums)
+        rgb_grad[...] = jnp.zeros_like(rgb_grad)
+
+    for half in range(TILE // 128):
+        for k, part in enumerate((d0, d1, d2, d3)):
+            rows = pl.ds(pl.multiple_of(jnp.bitwise_xor(me, k) * 128, 128), 128)
+            value = dot(part[:, half * 512 : (half + 1) * 512], order[...])
+            for phase in range(4):
+                fields[phase, rows, half * 128 : (half + 1) * 128] = value[:, phase * 128 : (phase + 1) * 128]
+
+    here = pl.ds(pl.multiple_of(j * TILE, TILE), TILE)
+    for phase in range(4):
+        noise_plain = noise[phase : phase + 1, here]
+        noise_row = gains[1] * noise_plain
+        cot_here = color_cot[phase, :, here]
+
+        @pl.loop(0, convolved.shape[1] // ROWS)
+        def _(i):
+            rows = pl.ds(pl.multiple_of(i * ROWS, ROWS), ROWS)
+            conv = convolved[phase, rows, :]
+            scale = wide(demod[rows, :])
+            style = wide(cols[2, rows, :])
+            pre = conv * scale + noise_row + wide(cols[4, rows, :])
+            sigma = jax.nn.sigmoid(pre)
+            act = root_two * (0.2 * pre + 0.8 * (pre * sigma))
+            slope = root_two * (0.2 + 0.8 * sigma * (1.0 + pre * (1.0 - sigma)))
+            back = dot(rgb_cols[rows, :], cot_here)
+            grad = (fields[phase, rows, :] * live + back * style) * slope
+            cot_two[phase, rows, :] = (grad * scale).astype(BF)
+            for_rgb[rows, :] = (act * style).astype(BF)
+            for n, value in enumerate((grad * conv, grad, grad * noise_plain, back * act)):
+                sums[n, rows, :] += value[:, :128] + value[:, 128:]
+
+        rgb_grad[...] += dot_nt(cot_here, for_rgb[...])
+
+    @pl.when(j == pl.num_programs(0) - 1)
+    def _():
+        scale = demod[...]
+        total = jnp.sum(sums[0], axis=1, keepdims=True)
+        inner[...] = -0.5 * scale * scale * scale * total
+
+
+def second_grad_kernel(ids, cot_two, scaled_two, full, inner, rows_ref, keep, send, copies, total):
+    t = pl.program_id(0)
+    me, core = ids[0], ids[1]
+
+    @pl.when(t == 0)
+    def _():
+        make_copies(cot_two, copies)
+
+    row_step, col_step = 1 - t // 3, 1 - t % 3
+    summed = None
+    for phase in range(4):
+        a, b = phase // 2, phase % 2
+        far_row = jnp.where(row_step == 2 * a - 1, 1, 0)
+        far_col = jnp.where(col_step == 2 * b - 1, 1, 0)
+        other_row = (a + row_step + 2) % 2
+        other_col = (b + col_step + 2) % 2
+        index = ((other_row * 2 + other_col) * 2 + far_row) * 2 + far_col
+        term = dot_nt(copies[index], scaled_two[phase])
+        summed = term if summed is None else summed + term
+    total[...] = summed
+    split_grad(me, core, total, full, t, inner, rows_ref[1:2, :], keep, send)
+
+
+def split_grad(me, core, total, full, t, inner, square_row, keep, send):
+    for k in range(4):
+        base = jnp.bitwise_xor(me, k) * 128
+        for out, part in ((keep, core), (send, 1 - core)):
+            rows = pl.ds(pl.multiple_of(base + part * 64, 64), 64)
+            column = jnp.concatenate([inner[rows, :]] * 4, axis=1)
+            weight = full[t, rows, :].astype(F32)
+            out[k, 0] = (total[rows, :] + (2.0 * weight) * (column * square_row)).astype(BF)
+
+
+def second_back_kernel(ids, gains, cot_two, full, raised, cols, demod, noise,
+                       cot_one, sums, inner, copies, turned, back):
+    j = pl.program_id(0)
+
+    @pl.when(j == 0)
+    def _():
+        sums[...] = jnp.zeros_like(sums)
+        make_copies(cot_two, copies)
+
+        @pl.loop(0, 9)
+        def _(t):
+            turned[t] = full[t].T
+
+    here = pl.ds(pl.multiple_of(j * TILE, TILE), TILE)
+    for phase in range(4):
+        total = None
+        for t in range(9):
+            term = dot(turned[t], copies[copy_index(phase, 1 - t // 3, 1 - t % 3), :, here])
+            total = term if total is None else total + term
+        back[...] = total
+        noise_plain = noise[phase : phase + 1, here]
+        noise_row = gains[0] * noise_plain
+
+        @pl.loop(0, back.shape[0] // ROWS)
+        def _(i):
+            rows = pl.ds(pl.multiple_of(i * ROWS, ROWS), ROWS)
+            conv = raised[phase, rows, :]
+            scale = wide(demod[rows, :])
+            pre = conv * scale + noise_row + wide(cols[3, rows, :])
+            sigma = jax.nn.sigmoid(pre)
+            act = root_two * (0.2 * pre + 0.8 * (pre * sigma))
+            slope = root_two * (0.2 + 0.8 * sigma * (1.0 + pre * (1.0 - sigma)))
+            value = back[rows, :]
+            grad = value * wide(cols[1, rows, :]) * slope
+            cot_one[phase, rows, :] = (grad * scale).astype(BF)
+            for n, item in enumerate((grad * conv, grad, grad * noise_plain, value * act)):
+                sums[n, rows, :] += item[:, :128] + item[:, 128:]
+
+    @pl.when(j == pl.num_programs(0) - 1)
+    def _():
+        scale = demod[...]
+        total = jnp.sum(sums[0], axis=1, keepdims=True)
+        inner[...] = -0.5 * scale * scale * scale * total
+
+
+def first_kernel(ids, cot_one, scaled_one, full, inner, cols, rows_ref, x0, x1, x2, x3,
+                 keep, send, b0, b1, b2, b3, sums, copies, total, back):
+    t = pl.program_id(0)
+    me, core = ids[0], ids[1]
+
+    @pl.when(t == 0)
+    def _():
+        back[...] = jnp.zeros_like(back)
+
+        @pl.loop(0, cot_one.shape[1] // 32)
+        def _(i):
+            rows = pl.ds(pl.multiple_of(i * 32, 32), 32)
+            for phase, (row_phase, col_phase) in enumerate(phase_pairs):
+                field = cot_one[phase, rows, :]
+                for k, r in phase_taps[row_phase]:
+                    for l, q in phase_taps[col_phase]:
+                        copies[3 * k + l, rows, :] = move(field, -r, -q)
+
+    total[...] = dot_nt(copies[t], scaled_one[...])
+    split_grad(me, core, total, full, t, inner, rows_ref[0:1, :], keep, send)
+    turned = full[t].T
+    for n in range(back.shape[1] // TILE):
+        here = slice(n * TILE, (n + 1) * TILE)
+        back[:, here] += dot(turned, copies[t, :, here])
+
+    @pl.when(t == pl.num_programs(0) - 1)
+    def _():
+        for k, (out, part) in enumerate(((b0, x0), (b1, x1), (b2, x2), (b3, x3))):
+            base = jnp.bitwise_xor(me, k) * 128
+
+            @pl.loop(0, 128 // 32)
+            def _(i):
+                rows = pl.ds(pl.multiple_of(base + i * 32, 32), 32)
+                here = pl.ds(pl.multiple_of(i * 32, 32), 32)
+                value = back[rows, :]
+                style = jnp.concatenate([cols[0, rows, :]] * 8, axis=1)
+                out[here, :] = (value * style).astype(out.dtype)
+                sums[rows, :] = jnp.broadcast_to(
+                    jnp.sum(value * part[here, :].astype(F32), axis=1, keepdims=True), (32, 128)
+                )
+
+
+def call(kernel, grid, ins, outs, scratch, args):
+    return pl.pallas_call(
+        kernel,
+        grid=(grid,),
+        in_specs=ins,
+        out_specs=[spec for _, _, spec in outs],
+        out_shape=[jax.ShapeDtypeStruct(shape, dtype) for shape, dtype, _ in outs],
+        scratch_shapes=scratch,
+        compiler_params=pltpu.CompilerParams(vmem_limit_bytes=LIMIT),
+    )(*args)
+
+
+def quad(value, k):
+    return lax.ppermute(value, "chan", [(i, i ^ k) for i in range(4)])
+
+
+def pair(value):
+    return lax.ppermute(value, "dp", [(i, i ^ 1) for i in range(8)])
+
+
+def after(value, *others):
+    return lax.optimization_barrier((value,) + others)[0]
+
+
+def natural(parts, me):
+    stacked = jnp.stack(parts)
+    stacked = stacked.reshape((2, 2) + stacked.shape[1:])
+    stacked = jnp.where(me % 2 == 1, stacked[:, ::-1], stacked)
+    stacked = jnp.where(me // 2 == 1, stacked[::-1], stacked)
+    return stacked.reshape((4,) + stacked.shape[2:])
+
+
+def pick(value, index, axis):
+    return lax.dynamic_index_in_dim(value, index, axis, keepdims=False)
+
+
+def to_phases(field):
+    lead = field.shape[:-1]
+    blocked = field.reshape(lead + (HALF, 2, HALF, 2))
+    n = len(lead)
+    return blocked.transpose((n + 1, n + 3) + tuple(range(n)) + (n, n + 2)).reshape((4,) + lead + (HALF * HALF,))
+
+
+def phase_order():
+    place = jnp.arange(512)
+    row, col = place // SIDE, place % SIDE
+    grouped = ((row % 2) * 2 + col % 2) * 128 + (row // 2) * HALF + col // 2
+    return (jnp.arange(512)[:, None] == grouped[None, :]).astype(BF)
+
+
+def image_body(
+    feat_in,
+    rgb_in,
+    latent,
+    noise_first,
+    noise_second,
+    live_count,
+    conv_first,
+    conv_second,
+    style_weight,
+    style_bias,
+    rgb_weight,
+    conv_bias,
+    rgb_bias,
+    noise_gain,
+    feat_grad,
+    rgb_grad,
+):
+    local_ch, images, half_pix = feat_in.shape
+    channels = 4 * local_ch
+    pixels = feat_grad.shape[2]
+    me = lax.axis_index("chan")
+    row = lax.axis_index("dp")
+    core = row % 2
+    depth = row // 2
+    to = [jnp.bitwise_xor(me, k) for k in range(4)]
+    live_mask = (jnp.arange(images) < live_count[0]).astype(F32)
+    live = (me < live_count[0]).astype(F32)
+    ids = jnp.stack([me, core]).astype(jnp.int32)
+    gains = jnp.concatenate([noise_gain, live[None]])
+
+    styles = jnp.einsum("bw,jwc->bjc", latent, style_weight, precision=precise) + style_bias[None]
+    shared = jnp.concatenate([conv_bias, rgb_weight.astype(F32)])
+    packs = [jnp.concatenate([pick(styles, to[k], 0), shared]) for k in range(4)]
+    packs = [packs[0]] + [quad(packs[k], k) for k in (1, 2, 3)]
+    vectors = natural(packs, me).transpose(1, 0, 2).reshape(8, channels)
+    style_mine, bias_all, rgb_all = vectors[:3], vectors[3:5], vectors[5:8]
+    cols = jnp.broadcast_to(vectors[:5, :, None], (5, channels, 128))
+    squares = jnp.pad(style_mine[:2] * style_mine[:2], ((0, 6), (0, 0)))
+
+    x = [pick(feat_in, to[k], 1) for k in range(4)]
+    x = [x[0]] + [quad(x[k], k) for k in (1, 2, 3)]
+
+    half_one = lax.dynamic_slice_in_dim(conv_first, core * 64, 64, 1)
+    half_two = lax.dynamic_slice_in_dim(conv_second, core * 64, 64, 1)
+    one_others = [quad(half_one, k) for k in (1, 2, 3)]
+    one_swapped = [pair(part) for part in one_others]
+    half_two = after(half_two, one_others[2])
+    two_others = [quad(half_two, k) for k in (1, 2, 3)]
+    two_swapped = [pair(part) for part in two_others]
+    d = [pick(feat_grad, to[k], 1) for k in range(4)]
+    d = [d[0]] + [quad(after(d[k], two_others[2]), k) for k in (1, 2, 3)]
+
+    noise_one = to_phases(pick(noise_first, me, 0))
+    noise_two = to_phases(pick(noise_second, me, 0))
+    order = phase_order()
+    cot_mine = (pick(rgb_grad, me, 0) * live).astype(BF)
+    color_cot = jnp.pad(to_phases(cot_mine), ((0, 0), (0, 13), (0, 0)))
+    rgb_rows = jnp.pad(rgb_all.astype(BF), ((0, 13), (0, 0)))
+    rgb_cols = rgb_rows.T
+
+    tiles = half_pix // TILE
+    vec = ((channels, 128), F32, whole((channels, 128)))
+    cols_spec, row_spec, noise_spec = whole(cols.shape), whole(squares.shape), whole(noise_one.shape)
+    full_spec = whole((9, channels, channels))
+    tile_spec = pl.BlockSpec((4, channels, TILE), lambda j: (0, 0, j))
+    field_spec = whole((4, channels, half_pix))
+    image_spec = pl.BlockSpec((local_ch, 4 * TILE), lambda j: (0, j))
+    x_spec = whole((local_ch, half_pix))
+
+    raised, scaled_two, full_one, scaled_one, demod_one = call(
+        up_kernel,
+        tiles,
+        [SMEM, SMEM] + [x_spec] * 4 + [ANY] * 7 + [cols_spec, row_spec, noise_spec],
+        [
+            ((4, channels, half_pix), F32, tile_spec),
+            ((4, channels, half_pix), BF, tile_spec),
+            ((9, channels, channels), BF, full_spec),
+            ((channels, half_pix), BF, whole((channels, half_pix))),
+            vec,
+        ],
+        [pltpu.VMEM((4, channels, half_pix), BF), pltpu.SemaphoreType.DMA((7,))],
+        (ids, gains, *x, conv_first, *one_others, *one_swapped, cols, squares, noise_one),
+    )
+
+    convolved, f0, f1, f2, f3, color, full_two, demod_two = call(
+        conv_kernel,
+        tiles,
+        [SMEM, SMEM, field_spec] + [ANY] * 7
+        + [cols_spec, row_spec, noise_spec, whole((512, 512)), whole((16, channels))],
+        [((4, channels, half_pix), F32, tile_spec)]
+        + [((local_ch, pixels), BF, image_spec)] * 4
+        + [
+            ((4, 16, half_pix), F32, pl.BlockSpec((4, 16, TILE), lambda j: (0, 0, j))),
+            ((9, channels, channels), BF, full_spec),
+            vec,
+        ],
+        [
+            pltpu.VMEM((16, channels, half_pix), BF),
+            pltpu.VMEM((TILE // 128, channels, 512), BF),
+            pltpu.VMEM((channels, TILE), BF),
+            pltpu.SemaphoreType.DMA((7,)),
+        ],
+        (ids, gains, scaled_two, conv_second, *two_others, *two_swapped, cols, squares, noise_two, order, rgb_rows),
+    )
+
+    cot_two, sums_two, rgb_part, inner_two = call(
+        cot_kernel,
+        tiles,
+        [SMEM, SMEM, tile_spec] + [image_spec] * 4
+        + [cols_spec, whole((channels, 128)), noise_spec, whole((512, 512)), whole((4, 16, half_pix)),
+           whole((channels, 16))],
+        [
+            ((4, channels, half_pix), BF, tile_spec),
+            ((4, channels, 128), F32, whole((4, channels, 128))),
+            ((16, channels), F32, whole((16, channels))),
+            vec,
+        ],
+        [pltpu.VMEM((4, channels, TILE), F32), pltpu.VMEM((channels, TILE), BF)],
+        (ids, gains, convolved, *d, cols, demod_two, noise_two, order.T, color_cot, rgb_cols),
+    )
+
+    grad_spec = pl.BlockSpec((4, 1, 64, channels), lambda t: (0, t, 0, 0))
+    grad_shape = ((4, 9, 64, channels), BF, grad_spec)
+    keep_two, send_two = call(
+        second_grad_kernel,
+        9,
+        [SMEM, field_spec, field_spec, full_spec, whole((channels, 128)), row_spec],
+        [grad_shape, grad_shape],
+        [pltpu.VMEM((16, channels, half_pix), BF), pltpu.VMEM((channels, channels), F32)],
+        (ids, cot_two, scaled_two, full_two, inner_two, squares),
+    )
+    grad_two = reduce_grad(keep_two, send_two, me, depth)
+
+    cot_one, sums_one, inner_one = call(
+        second_back_kernel,
+        tiles,
+        [SMEM, SMEM, field_spec, full_spec, tile_spec, cols_spec, whole((channels, 128)), noise_spec],
+        [
+            ((4, channels, half_pix), BF, tile_spec),
+            ((4, channels, 128), F32, whole((4, channels, 128))),
+            vec,
+        ],
+        [
+            pltpu.VMEM((16, channels, half_pix), BF),
+            pltpu.VMEM((9, channels, channels), BF),
+            pltpu.VMEM((channels, TILE), F32),
+        ],
+        (ids, gains, cot_two, full_two, raised, cols, demod_one, noise_one),
+    )
+
+    keep_one, send_one, b0, b1, b2, b3, sums_zero = call(
+        first_kernel,
+        9,
+        [SMEM, field_spec, whole((channels, half_pix)), full_spec, whole((channels, 128)), cols_spec, row_spec]
+        + [x_spec] * 4,
+        [grad_shape, grad_shape] + [((local_ch, half_pix), BF, x_spec)] * 4 + [vec],
+        [
+            pltpu.VMEM((9, channels, half_pix), BF),
+            pltpu.VMEM((channels, channels), F32),
+            pltpu.VMEM((channels, half_pix), F32),
+        ],
+        (ids, cot_one, scaled_one, full_one, inner_one, cols, squares, *x),
+    )
+    grad_one = reduce_grad(keep_one, send_one, me, depth)
+
+    feat_out = [f0] + [quad(after(part, d[3]), k + 1) for k, part in enumerate((f1, f2, f3))]
+    feat_out = natural(feat_out, me).transpose(1, 0, 2)
+    back = [b0] + [quad(part, k + 1) for k, part in enumerate((b1, b2, b3))]
+    feat_in_grad = natural(back, me).transpose(1, 0, 2).astype(F32)
+
+    lift_matrix = upsample_matrix(HALF)
+    color = color[:, :3].reshape(2, 2, 3, HALF, HALF).transpose(2, 3, 0, 4, 1).reshape(3, pixels)
+    shard_pix = pixels // 4
+    color = color.reshape(3, 4, shard_pix)
+    color = [pick(color, to[k], 1) for k in range(4)]
+    color = natural([color[0]] + [quad(color[k], k) for k in (1, 2, 3)], me)
+    skip_up = jnp.einsum(
+        "up,bkpq,vq->bkuv",
+        lift_matrix,
+        rgb_in.reshape(images, 3, HALF, HALF),
+        lift_matrix,
+        precision=precise,
+    ).reshape(images, 3, pixels)
+    skip_mine = lax.dynamic_slice_in_dim(skip_up, me * shard_pix, shard_pix, 2)
+    rgb_out = (color + rgb_bias[None, :, None] + skip_mine) * live_mask[:, None, None]
+    rgb_cot = rgb_grad * live_mask[:, None, None]
+    rgb_in_grad = jnp.einsum(
+        "up,bkuv,vq->bkpq",
+        lift_matrix,
+        rgb_cot.reshape(images, 3, SIDE, SIDE),
+        lift_matrix,
+        precision=precise,
+    ).reshape(images, 3, half_pix)
+    rgb_bias_part = jnp.sum(rgb_cot, axis=(0, 2))
+
+    sums_two = jnp.sum(sums_two, axis=2)
+    sums_one = jnp.sum(sums_one, axis=2)
+    inner_two, inner_one = inner_two[:, 0], inner_one[:, 0]
+    style_two_demod = 2.0 * style_mine[1] * square_back(inner_two, full_two)
+    style_one_demod = 2.0 * style_mine[0] * square_back(inner_one, full_one)
+    rows_out = jnp.stack(
+        [
+            sums_zero[:, 0] + style_one_demod,
+            sums_one[3] + style_two_demod,
+            sums_two[3],
+            sums_one[1],
+            sums_two[1],
+            sums_one[2],
+            sums_two[2],
+        ]
+    )
+    rows_out = jnp.concatenate([rows_out, rgb_part[:3]]).reshape(10, 4, local_ch)
+    rows_out = [pick(rows_out, to[k], 1) for k in range(4)]
+    rows_in = natural([rows_out[0]] + [quad(rows_out[k], k) for k in (1, 2, 3)], me)
+    style_grads = rows_in[:, :3]
+    latent_part = jnp.einsum("bjc,jwc->bw", style_grads, style_weight, precision=precise)
+    latent_grad = latent_part + quad(latent_part, 1) + quad(latent_part, 2) + quad(latent_part, 3)
+    extra = jnp.pad(rgb_bias_part[None], ((0, 0), (0, local_ch - 3)))
+    gathered = jnp.concatenate([rows_in.reshape(40, local_ch), extra, latent.reshape(16, 128)])
+    gathered = lax.all_gather(gathered, "dp")
+    every_row = gathered[:, :40].reshape(8, 4, 10, local_ch)
+    every_latent = gathered[:, 41:].reshape(8, 4, 512)
+    style_weight_grad = jnp.einsum("gbw,gbjc->jwc", every_latent, every_row[:, :, :3], precision=precise)
+    summed = jnp.sum(every_row, axis=(0, 1))
+    gain_part = jnp.sum(summed[5:7], axis=1)
+    gain_grad = lax.psum(gain_part, "chan")
+    rgb_bias_grad = jnp.sum(gathered[:, 40, :3], axis=0)
+    return (
+        feat_out,
+        rgb_out,
+        feat_in_grad,
+        rgb_in_grad,
+        latent_grad,
+        grad_one,
+        grad_two,
+        style_weight_grad,
+        summed[:3],
+        summed[7:10],
+        summed[3:5],
+        rgb_bias_grad,
+        gain_grad,
+    )
+
+
+def square_back(inner, full):
+    total = jnp.zeros(full.shape[1:], F32)
+    for t in range(9):
+        value = full[t].astype(F32)
+        total = total + value * value
+    return jnp.sum(inner[:, None] * total, axis=0)
+
+
+def reduce_grad(keep, send, me, depth):
+    part = (keep.astype(F32) + pair(send).astype(F32)).astype(BF)
+    total = part[0].astype(F32)
+    for k in (1, 2, 3):
+        total = total + quad(part[k], k).astype(F32)
+    block = total.astype(BF).reshape(9, 4, 16, 512)
+
+    def along(value, k):
+        return lax.ppermute(value, "dp", [(i, i ^ (2 * k)) for i in range(8)])
+
+    summed = pick(block, depth, 1).astype(F32)
+    for k in (1, 2, 3):
+        summed = summed + along(pick(block, jnp.bitwise_xor(depth, k), 1), k).astype(F32)
+    summed = summed.astype(BF)
+    spread = natural([summed] + [along(summed, k) for k in (1, 2, 3)], depth)
+    mine = spread.transpose(1, 0, 2, 3).reshape(9, 64, 512)
+    theirs = pair(mine)
+    core = lax.axis_index("dp") % 2
+    low = jnp.where(core == 0, mine, theirs)
+    high = jnp.where(core == 0, theirs, mine)
+    return jnp.concatenate([low, high], axis=1).astype(F32)
+
+
 def solution(mesh):
+    alone = mesh.shape["chan"] == 4 and mesh.shape["dp"] == 8
     return jax.shard_map(
-        body,
+        image_body if alone else body,
         mesh=mesh,
         in_specs=(
             P("chan", "dp", None),

time: 1100 us -> 579 us (0.53)
  waiting for transfers between devices: 599 us -> 118 us
  Pallas kernels: 0 us -> 239 us
  matrix products: 209 us -> 8.7 us
  local copies, waits for them, and re-layouts: 154 us -> 83.9 us
  starting transfers between devices: 0.33 us -> 69 us
  other arithmetic: 68.3 us -> 26.6 us
  blocking collectives: 44.1 us -> 24.5 us
  between operations: 16.1 us -> 2.72 us
    reduce_scatter x2 -> x0, waiting for transfers between devices: 323 us -> none  [the longest x1 287 us: body(): lax.psum_scatter(jnp.einsum('toc,tobp->cbp', columns, taps_two, preferred...]
    pallas_call x0 -> x6, Pallas kernels: none -> 239 us  [call(): pl.pallas_call(kernel, grid=(grid,), in_specs=ins, out_specs=[spec for _,...]
    dot_general x38 -> x7, matrix products: 209 us -> 8.7 us  [the longest x2 3.92 us: image_body(): jnp.einsum('up,bkuv,vq->bkpq', lift_matrix, rgb_cot.reshape(images, 3, SI...]
    all_gather x2 -> x0, waiting for transfers between devices: 172 us -> none  [the longest x1 132 us: body(): gathered_two = lax.all_gather(scaled_two, 'chan', axis=0, tiled=True)]
    ppermute x0 -> x58, waiting for transfers between devices: none -> 118 us  [the longest x36 98.4 us: quad(): return lax.ppermute(value, 'chan', [(i, i ^ k) for i in range(4)])]
    psum x1 -> x0, waiting for transfers between devices: 89.6 us -> none  [body(): lax.psum((conv_one_grad, conv_two_grad, style_weight_part, style_bias_par...]
    ppermute x0 -> x58, starting transfers between devices: none -> 69 us  [the longest x36 44.6 us: quad(): return lax.ppermute(value, 'chan', [(i, i ^ k) for i in range(4)])]
    slice x19 -> x11, local copies, waits for them, and re-layouts: 72.4 us -> 4.78 us  [the longest x2 1.23 us: image_body(): inner_two, inner_one = (inner_two[:, 0], inner_one[:, 0])]
  transfers between devices with their start and end apart: 8 -> 58, of which waited for: 6 -> 19; matrix products, arithmetic and copies ran while one was open for 15% -> 19% of each run, Pallas kernels for 0% -> 21%
where the time goes in v1:
time: 579 us; the launch traced here: 573 us
  Pallas kernels  239 us (41%)
  waiting for transfers between devices  118 us (20%)
  local copies, waits for them, and re-layouts  83.9 us (14%)
  starting transfers between devices  69 us (12%)
  other arithmetic  26.6 us (5%)
  blocking collectives  24.5 us (4%)
  matrix products  8.7 us (2%)
    pallas_call x6, Pallas kernels, call(): pl.pallas_call(kernel, grid=(grid,), in_specs=ins, out_specs=[spec for _,...  239 us
    ppermute x36, waiting for transfers between devices, quad(): return lax.ppermute(value, 'chan', [(i, i ^ k) for i in range(4)])  98.4 us
    ppermute x36, starting transfers between devices, quad(): return lax.ppermute(value, 'chan', [(i, i ^ k) for i in range(4)])  44.6 us
    ppermute x12, starting transfers between devices, along(): return lax.ppermute(value, 'dp', [(i, i ^ 2 * k) for i in range(8)])  22.6 us
    dynamic_slice x4, local copies, waits for them, and re-layouts, pick(): return lax.dynamic_index_in_dim(value, index, axis, keepdims=False)  20.3 us
    ppermute x12, waiting for transfers between devices, along(): return lax.ppermute(value, 'dp', [(i, i ^ 2 * k) for i in range(8)])  19.9 us
    all_gather x1, blocking collectives, image_body(): gathered = lax.all_gather(gathered, 'dp')  14.4 us
    unnamed x70, local copies, waits for them, and re-layouts  12.3 us
  transfers between devices with their start and end apart: 58, of which 19 were waited for; matrix products, arithmetic and copies ran while one was open for 19% of the time, Pallas kernels for 21%

profile of v1, /device:TPU:0, one launch (start us, length us, event | category | flops | bytes accessed | tf_op | source)
XLA Modules:
  0.0 572.9 jit_solution(11696727820266795391)
XLA Ops:
  2.7 3.9 collective-permute-start.5
  20.8 16.4 %constant_dynamic-slice_fusion.4 = (bf16[128,1,4096]{2,1,0:T(2,128)(2,1)S(1)}, bf16[128,1,4096]{2,1,0:T(2,128)(2,1)}, bf16[128,1,4096]{2,1,0:T(2,128)(2,1)S(1)}, bf16[128,1,4096]{2,1,0:T(2,128)(2,1)S(1)}) fusion(bf16[128,4,4096]{2,1,0:T(4,128)(2,1)} %param.30, s32[]{:T(128)S(6)} %select_n.341, s32[]{:T(128)S(6)} %select_n.340, s32[]{:T(128)S(6)} %select_n.339, ...), kind=kLoop, calls=%fused_computation.130 | loop fusion | bytes 8388624 | tf_op jit(solution)/shard_map/jit(dynamic_index_in_dim)/dynamic_slice | solution.py:683
  69.3 3.7 copy.210
  74.8 8.6 %collective-permute-done.14.g3 = bf16[9,64,512]{2,1,0:T(8,128)(2,1)} collective-permute-done((bf16[9,64,512]{2,1,0:T(8,128)(2,1)}, bf16[9,64,512]{2,1,0:T(8,128)(2,1)}, u32[]{:S(2)}, u32[]{:S(2)}) %collective-permute-start.14) | collective-permute-done | bytes 589856 | tf_op jit(solution)/shard_map/ppermute | solution.py:663
  84.0 7.2 %collective-permute-done.12.g1 = bf16[9,64,512]{2,1,0:T(8,128)(2,1)} collective-permute-done((bf16[9,64,512]{2,1,0:T(8,128)(2,1)}, bf16[9,64,512]{2,1,0:T(8,128)(2,1)}, u32[]{:S(2)}, u32[]{:S(2)}) %collective-permute-start.12) | collective-permute-done | bytes 589856 | tf_op jit(solution)/shard_map/ppermute | solution.py:663
  98.4 26.4 %shard_map.255 = (f32[4,512,1024]{2,1,0:T(8,128)}, bf16[4,512,1024]{2,1,0:T(8,128)(2,1)}, bf16[9,512,512]{2,1,0:T(8,128)(2,1)}, bf16[512,1024]{1,0:T(8,128)(2,1)}, f32[512,128]{1,0:T(8,128)}) custom-call(s32[2]{0:T(128)} %pad_add_fusion.ids, f32[3]{0:T(128)} %pad_maximum_fusion.15.gains, bf16[128,1024]{1,0:T(8,128)(2,1)} %bitcast.274, ...), custom_call_target="tpu_custom_call" | custom-call | tf_op jit(solution)/shard_map/pallas_call | solution.py:651
  124.9 62.8 %shard_map.256 = (f32[4,512,1024]{2,1,0:T(8,128)}, bf16[128,4096]{1,0:T(8,128)(2,1)}, bf16[128,4096]{1,0:T(8,128)(2,1)}, bf16[128,4096]{1,0:T(8,128)(2,1)}, bf16...) custom-call(s32[2]{0:T(128)} %pad_add_fusion.ids, ...), custom_call_target="tpu_custom_call" | custom-call | tf_op jit(solution)/shard_map/pallas_call | solution.py:651
  201.2 4.6 convert_element_type.221
  217.7 29.2 %shard_map.257 = (bf16[4,512,1024]{2,1,0:T(8,128)(2,1)}, f32[4,512,128]{2,1,0:T(8,128)}, f32[16,512]{1,0:T(8,128)}, f32[512,128]{1,0:T(8,128)}) custom-call(s32[2]{0:T(128)} %pad_add_fusion.ids, f32[3]{0:T(128)} %pad_maximum_fusion.15.gains, f32[4,512,1024]{2,1,0:T(8,128)} %get-tuple-element.60.convolved, bf16[128,4096]{1,0:T(8,128)(2,1)} %bitcast.261, ...), custom_call_target="tpu_custom_call" | custom-call | tf_op jit(solution)/shard_map/pallas_call | solution.py:651
  246.9 62.9 %shard_map.258 = (bf16[4,512,1024]{2,1,0:T(8,128)(2,1)}, f32[4,512,128]{2,1,0:T(8,128)}, f32[512,128]{1,0:T(8,128)}) custom-call(s32[2]{0:T(128)} %pad_add_fusion.ids, f32[3]{0:T(128)} %pad_maximum_fusion.15.gains, bf16[4,512,1024]{2,1,0:T(8,128)(2,1)} %get-tuple-element.64.cot_two, bf16[9,512,512]{2,1,0:T(8,128)(2,1)} %get-tuple-element.65.full, ...), custom_call_target="tpu_custom_call" | custom-call | tf_op jit(solution)/shard_map/pallas_call | solution.py:651
  314.6 24.3 %shard_map.259 = (bf16[4,9,64,512]{3,2,1,0:T(8,128)(2,1)}, bf16[4,9,64,512]{3,2,1,0:T(8,128)(2,1)}, bf16[128,1024]{1,0:T(8,128)(2,1)}, bf16[128,1024]{1,0:T(8,12...) custom-call(s32[2]{0:T(128)} %pad_add_fusion.ids, ...), custom_call_target="tpu_custom_call" | custom-call | tf_op jit(solution)/shard_map/pallas_call | solution.py:651
  347.6 33.4 %shard_map.260 = (bf16[4,9,64,512]{3,2,1,0:T(8,128)(2,1)}, bf16[4,9,64,512]{3,2,1,0:T(8,128)(2,1)}) custom-call(s32[2]{0:T(128)} %pad_add_fusion.ids, bf16[4,512,1024]{2,1,0:T(8,128)(2,1)} %get-tuple-element.64.cot_two, bf16[4,512,1024]{2,1,0:T(8,128)(2,1)} %get-tuple-element.49.scaled_two, bf16[9,512,512]{2,1,0:T(8,128)(2,1)} %get-tuple-element.65.full, ...), custom_call_target="tpu_custom_call" | custom-call | tf_op jit(solution)/shard_map/pallas_call | solution.py:651
  387.2 14.4 %all-gather.1 = f32[8,57,128]{2,1,0:T(8,128)S(1)} all-gather(f32[1,57,128]{2,1,0:T(8,128)S(1)} %fusion.26), channel_id=2, replica_groups=mesh['dp'=8,'chan'=4] {'dp'}, dimensions={0}, use_global_device_ids=true | all-gather | bytes 262656 | tf_op jit(solution)/shard_map/all_gather | solution.py:920
  407.9 10.1 %psum.7 = f32[2]{0:T(128)} all-reduce(f32[2]{0:T(128)S(1)} %get-tuple-element.175), channel_id=1, replica_groups=mesh['dp'=8,'chan'=4] {'chan'}, use_global_device_ids=true, to_apply=%region_9.10 | all-reduce | flops 2 | bytes 16 | tf_op jit(solution)/shard_map/psum | solution.py:926
  426.9 19.4 %collective-permute-done.21 = bf16[128,4096]{1,0:T(8,128)(2,1)S(1)} collective-permute-done((bf16[128,4096]{1,0:T(8,128)(2,1)}, bf16[128,4096]{1,0:T(8,128)(2,1)S(1)}, u32[]{:S(2)}, u32[]{:S(2)}) %collective-permute-start.21) | collective-permute-done | bytes 1048608 | tf_op jit(solution)/shard_map/ppermute | solution.py:663
  446.3 17.6 %collective-permute-done.20 = bf16[128,4096]{1,0:T(8,128)(2,1)S(1)} collective-permute-done((bf16[128,4096]{1,0:T(8,128)(2,1)}, bf16[128,4096]{1,0:T(8,128)(2,1)S(1)}, u32[]{:S(2)}, u32[]{:S(2)}) %collective-permute-start.20) | collective-permute-done | bytes 1048608 | tf_op jit(solution)/shard_map/ppermute | solution.py:663
  475.9 8.9 %collective-permute-done.48 = bf16[9,64,512]{2,1,0:T(8,128)(2,1)S(1)} collective-permute-done((bf16[9,64,512]{2,1,0:T(8,128)(2,1)S(1)}, bf16[9,64,512]{2,1,0:T(8,128)(2,1)S(1)}, u32[]{:S(2)}, u32[]{:S(2)}) %collective-permute-start.48) | collective-permute-done | bytes 589856 | tf_op jit(solution)/shard_map/ppermute | solution.py:663
  487.2 11.0 %collective-permute-done.50 = bf16[9,64,512]{2,1,0:T(8,128)(2,1)S(1)} collective-permute-done((bf16[9,64,512]{2,1,0:T(8,128)(2,1)S(1)}, bf16[9,64,512]{2,1,0:T(8,128)(2,1)S(1)}, u32[]{:S(2)}, u32[]{:S(2)}) %collective-permute-start.50) | collective-permute-done | bytes 589856 | tf_op jit(solution)/shard_map/ppermute | solution.py:663
  503.5 6.5 %collective-permute-done.37 = bf16[9,64,512]{2,1,0:T(8,128)(2,1)S(1)} collective-permute-done((bf16[9,64,512]{2,1,0:T(8,128)(2,1)S(1)}, bf16[9,64,512]{2,1,0:T(8,128)(2,1)S(1)}, u32[]{:S(2)}, u32[]{:S(2)}) %collective-permute-start.37) | collective-permute-done | bytes 589856 | tf_op jit(solution)/shard_map/ppermute | solution.py:663
  510.7 10.7 %collective-permute-done.39 = bf16[9,64,512]{2,1,0:T(8,128)(2,1)S(1)} collective-permute-done((bf16[9,64,512]{2,1,0:T(8,128)(2,1)S(1)}, bf16[9,64,512]{2,1,0:T(8,128)(2,1)S(1)}, u32[]{:S(2)}, u32[]{:S(2)}) %collective-permute-start.39) | collective-permute-done | bytes 589856 | tf_op jit(solution)/shard_map/ppermute | solution.py:663
  534.4 10.3 %collective-permute-done.41 = bf16[9,16,512]{2,1,0:T(8,128)(2,1)S(1)} collective-permute-done((bf16[9,16,512]{2,1,0:T(8,128)(2,1)S(1)}, bf16[9,16,512]{2,1,0:T(8,128)(2,1)S(1)}, u32[]{:S(2)}, u32[]{:S(2)}) %collective-permute-start.41) | collective-permute-done | bytes 147488 | tf_op jit(solution)/shard_map/ppermute | solution.py:961
  547.4 7.4 %collective-permute-start.43 = (bf16[9,16,512]{2,1,0:T(8,128)(2,1)S(1)}, bf16[9,16,512]{2,1,0:T(8,128)(2,1)S(1)}, u32[]{:S(2)}, u32[]{:S(2)}) collective-permute-start(bf16[9,16,512]{2,1,0:T(8,128)(2,1)S(1)} %fusion.17), channel_id=1, source_target_pairs={{0,8},{4,12},{8,0},{12,4},{16,24},{20,28},{24,16},{28,20},{1,9},{5... | collective-permute-start | bytes 442376 | tf_op jit(solution)/shard_map/ppermute | solution.py:961
  558.0 4.1 collective-permute-done.44
  563.5 5.3 copy.208
  (302 shorter events, 161.1 us)
Async XLA Ops:
  2.7 44.8 %collective-permute-start.5 = (bf16[9,64,512]{2,1,0:T(8,128)(2,1)}, bf16[9,64,512]{2,1,0:T(8,128)(2,1)}, u32[]{:S(2)}, u32[]{:S(2)}) collective-permute-start(bf16[9,64,512]{2,1,0:T(8,128)(2,1)} %constant_dynamic-slice_fusion.16), channel_id=1, source_target_pairs={{0,3},{1,2},{2,1},{3,0},{4,7},{5,6},{6,5},{7,4},{8,11},{9,10},{10,... | collective-permute-start | bytes 1769480 | tf_op jit(solution)/shard_map/ppermute | solution.py:663
  6.6 53.2 %collective-permute-start.4 = (bf16[9,64,512]{2,1,0:T(8,128)(2,1)}, bf16[9,64,512]{2,1,0:T(8,128)(2,1)}, u32[]{:S(2)}, u32[]{:S(2)}) collective-permute-start(bf16[9,64,512]{2,1,0:T(8,128)(2,1)} %constant_dynamic-slice_fusion.16), channel_id=1, source_target_pairs={{0,2},{1,3},{2,0},{3,1},{4,6},{5,7},{6,4},{7,5},{8,10},{9,11},{10,... | collective-permute-start | bytes 1769480 | tf_op jit(solution)/shard_map/ppermute | solution.py:663
  9.8 32.7 %collective-permute-start.9 = (f32[8,128]{1,0:T(8,128)S(1)}, f32[8,128]{1,0:T(8,128)S(1)}, u32[]{:S(2)}, u32[]{:S(2)}) collective-permute-start(f32[8,128]{1,0:T(8,128)S(1)} %get-tuple-element.190), channel_id=1, source_target_pairs={{0,1},{1,0},{2,3},{3,2},{4,5},{5,4},{6,7},{7,6},{8,9},{9,8},{10,11... | collective-permute-start | bytes 12296 | tf_op jit(solution)/shard_map/ppermute | solution.py:663
  13.6 40.7 %collective-permute-start = (bf16[128,1024]{1,0:T(8,128)(2,1)}, bf16[128,1024]{1,0:T(8,128)(2,1)}, u32[]{:S(2)}, u32[]{:S(2)}) collective-permute-start(bf16[128,1024]{1,0:T(8,128)(2,1)} %bitcast.244), channel_id=1, source_target_pairs={{0,1},{1,0},{2,3},{3,2},{4,5},{5,4},{6,7},{7,6},{8,9},{9,8},{10,11... | collective-permute-start | bytes 786440 | tf_op jit(solution)/shard_map/ppermute | solution.py:663
  16.4 39.8 %collective-permute-start.1 = (bf16[128,1024]{1,0:T(8,128)(2,1)}, bf16[128,1024]{1,0:T(8,128)(2,1)}, u32[]{:S(2)}, u32[]{:S(2)}) collective-permute-start(bf16[128,1024]{1,0:T(8,128)(2,1)} %bitcast.243), channel_id=1, source_target_pairs={{0,2},{1,3},{2,0},{3,1},{4,6},{5,7},{6,4},{7,5},{8,10},{9,11},{10,... | collective-permute-start | bytes 786440 | tf_op jit(solution)/shard_map/ppermute | solution.py:663
  59.3 31.9 %collective-permute-start.12 = (bf16[9,64,512]{2,1,0:T(8,128)(2,1)}, bf16[9,64,512]{2,1,0:T(8,128)(2,1)}, u32[]{:S(2)}, u32[]{:S(2)}) collective-permute-start(bf16[9,64,512]{2,1,0:T(8,128)(2,1)} %constant_dynamic-slice_fusion.11), channel_id=1, source_target_pairs={{0,1},{1,0},{2,3},{3,2},{4,5},{5,4},{6,7},{7,6},{8,9},{9,8},{10,11... | collective-permute-start | bytes 1769480 | tf_op jit(solution)/shard_map/ppermute | solution.py:663
  91.2 33.7 %collective-permute-start.16 = (bf16[9,64,512]{2,1,0:T(8,128)(2,1)}, bf16[9,64,512]{2,1,0:T(8,128)(2,1)}, u32[]{:S(2)}, u32[]{:S(2)}) collective-permute-start(bf16[9,64,512]{2,1,0:T(8,128)(2,1)} %collective-permute-done.13.g2), channel_id=1, source_target_pairs={{0,4},{4,0},{8,12},{12,8},{16,20},{20,16},{24,28},{28,24},{1,5},{5... | collective-permute-start | bytes 1769480 | tf_op jit(solution)/shard_map/ppermute | solution.py:667
  91.2 33.7 %collective-permute-start.15 = (bf16[9,64,512]{2,1,0:T(8,128)(2,1)}, bf16[9,64,512]{2,1,0:T(8,128)(2,1)}, u32[]{:S(2)}, u32[]{:S(2)}) collective-permute-start(bf16[9,64,512]{2,1,0:T(8,128)(2,1)} %collective-permute-done.12.g1), channel_id=1, source_target_pairs={{0,4},{4,0},{8,12},{12,8},{16,20},{20,16},{24,28},{28,24},{1,5},{5... | collective-permute-start | bytes 1769480 | tf_op jit(solution)/shard_map/ppermute | solution.py:667
  91.7 126.0 %collective-permute-start.25 = (bf16[128,4096]{1,0:T(8,128)(2,1)}, bf16[128,4096]{1,0:T(8,128)(2,1)}, u32[]{:S(2)}, u32[]{:S(2)}) collective-permute-start(bf16[128,4096]{1,0:T(8,128)(2,1)} %bitcast.279), channel_id=1, source_target_pairs={{0,1},{1,0},{2,3},{3,2},{4,5},{5,4},{6,7},{7,6},{8,9},{9,8},{10,11... | collective-permute-start | bytes 3145736 | tf_op jit(solution)/shard_map/ppermute | solution.py:663
  92.3 125.4 %collective-permute-start.26 = (bf16[128,4096]{1,0:T(8,128)(2,1)}, bf16[128,4096]{1,0:T(8,128)(2,1)}, u32[]{:S(2)}, u32[]{:S(2)}) collective-permute-start(bf16[128,4096]{1,0:T(8,128)(2,1)} %get-tuple-element.62), channel_id=1, source_target_pairs={{0,2},{1,3},{2,0},{3,1},{4,6},{5,7},{6,4},{7,5},{8,10},{9,11},{10,... | collective-permute-start | bytes 3145736 | tf_op jit(solution)/shard_map/ppermute | solution.py:663
  93.6 124.1 %collective-permute-start.18 = (bf16[128,4096]{1,0:T(8,128)(2,1)}, bf16[128,4096]{1,0:T(8,128)(2,1)}, u32[]{:S(2)}, u32[]{:S(2)}) collective-permute-start(bf16[128,4096]{1,0:T(8,128)(2,1)} %get-tuple-element.53), channel_id=1, source_target_pairs={{0,3},{1,2},{2,1},{3,0},{4,7},{5,6},{6,5},{7,4},{8,11},{9,10},{10,... | collective-permute-start | bytes 3145736 | tf_op jit(solution)/shard_map/ppermute | solution.py:663
  342.5 40.7 %collective-permute-start.30 = (f32[10,128]{1,0:T(8,128)S(1)}, f32[10,128]{1,0:T(8,128)S(1)}, u32[]{:S(2)}, u32[]{:S(2)}) collective-permute-start(f32[10,128]{1,0:T(8,128)S(1)} %bitcast.314), channel_id=1, source_target_pairs={{0,1},{1,0},{2,3},{3,2},{4,5},{5,4},{6,7},{7,6},{8,9},{9,8},{10,11... | collective-permute-start | bytes 15368 | tf_op jit(solution)/shard_map/ppermute | solution.py:663
  344.1 40.4 %collective-permute-start.31 = (f32[10,128]{1,0:T(8,128)S(1)}, f32[10,128]{1,0:T(8,128)S(1)}, u32[]{:S(2)}, u32[]{:S(2)}) collective-permute-start(f32[10,128]{1,0:T(8,128)S(1)} %bitcast.313), channel_id=1, source_target_pairs={{0,2},{1,3},{2,0},{3,1},{4,6},{5,7},{6,4},{7,5},{8,10},{9,11},{10,... | collective-permute-start | bytes 15368 | tf_op jit(solution)/shard_map/ppermute | solution.py:663
  344.8 39.8 %collective-permute-start.32 = (f32[10,128]{1,0:T(8,128)S(1)}, f32[10,128]{1,0:T(8,128)S(1)}, u32[]{:S(2)}, u32[]{:S(2)}) collective-permute-start(f32[10,128]{1,0:T(8,128)S(1)} %bitcast.312), channel_id=1, source_target_pairs={{0,3},{1,2},{2,1},{3,0},{4,7},{5,6},{6,5},{7,4},{8,11},{9,10},{10,... | collective-permute-start | bytes 15368 | tf_op jit(solution)/shard_map/ppermute | solution.py:663
  381.0 38.6 %collective-permute-start.27 = (bf16[128,1024]{1,0:T(8,128)(2,1)}, bf16[128,1024]{1,0:T(8,128)(2,1)S(1)}, u32[]{:S(2)}, u32[]{:S(2)}) collective-permute-start(bf16[128,1024]{1,0:T(8,128)(2,1)} %get-tuple-element.73), channel_id=1, source_target_pairs={{0,1},{1,0},{2,3},{3,2},{4,5},{5,4},{6,7},{7,6},{8,9},{9,8},{10,11... | collective-permute-start | bytes 786440 | tf_op jit(solution)/shard_map/ppermute | solution.py:663
  382.5 37.9 %collective-permute-start.28 = (bf16[128,1024]{1,0:T(8,128)(2,1)}, bf16[128,1024]{1,0:T(8,128)(2,1)S(1)}, u32[]{:S(2)}, u32[]{:S(2)}) collective-permute-start(bf16[128,1024]{1,0:T(8,128)(2,1)} %get-tuple-element.74), channel_id=1, source_target_pairs={{0,2},{1,3},{2,0},{3,1},{4,6},{5,7},{6,4},{7,5},{8,10},{9,11},{10,... | collective-permute-start | bytes 786440 | tf_op jit(solution)/shard_map/ppermute | solution.py:663
  383.2 39.4 %collective-permute-start.29 = (bf16[128,1024]{1,0:T(8,128)(2,1)S(1)}, bf16[128,1024]{1,0:T(8,128)(2,1)S(1)}, u32[]{:S(2)}, u32[]{:S(2)}) collective-permute-start(bf16[128,1024]{1,0:T(8,128)(2,1)S(1)} %copy-done.18), channel_id=1, source_target_pairs={{0,3},{1,2},{2,1},{3,0},{4,7},{5,6},{6,5},{7,4},{8,11},{9,10},{10,... | collective-permute-start | bytes 786440 | tf_op jit(solution)/shard_map/ppermute | solution.py:663
  384.5 80.3 %collective-permute-start.47 = (bf16[4,9,64,512]{3,2,1,0:T(8,128)(2,1)}, bf16[4,9,64,512]{3,2,1,0:T(8,128)(2,1)}, u32[]{:S(2)}, u32[]{:S(2)}) collective-permute-start(bf16[4,9,64,512]{3,2,1,0:T(8,128)(2,1)} %get-tuple-element.84), channel_id=1, source_target_pairs={{0,4},{4,0},{8,12},{12,8},{16,20},{20,16},{24,28},{28,24},{1,5},{5... | collective-permute-start | bytes 7077896 | tf_op jit(solution)/shard_map/ppermute | solution.py:667
  419.6 44.4 %collective-permute-start.20 = (bf16[128,4096]{1,0:T(8,128)(2,1)}, bf16[128,4096]{1,0:T(8,128)(2,1)S(1)}, u32[]{:S(2)}, u32[]{:S(2)}) collective-permute-start(bf16[128,4096]{1,0:T(8,128)(2,1)} %get-tuple-element.56), channel_id=1, source_target_pairs={{0,2},{1,3},{2,0},{3,1},{4,6},{5,7},{6,4},{7,5},{8,10},{9,11},{10,... | collective-permute-start | bytes 3145736 | tf_op jit(solution)/shard_map/ppermute | solution.py:663
  420.4 43.6 %collective-permute-start.19 = (bf16[128,4096]{1,0:T(8,128)(2,1)}, bf16[128,4096]{1,0:T(8,128)(2,1)S(1)}, u32[]{:S(2)}, u32[]{:S(2)}) collective-permute-start(bf16[128,4096]{1,0:T(8,128)(2,1)} %get-tuple-element.54), channel_id=1, source_target_pairs={{0,1},{1,0},{2,3},{3,2},{4,5},{5,4},{6,7},{7,6},{8,9},{9,8},{10,11... | collective-permute-start | bytes 3145736 | tf_op jit(solution)/shard_map/ppermute | solution.py:663
  422.6 49.3 %collective-permute-start.36 = (bf16[4,9,64,512]{3,2,1,0:T(8,128)(2,1)}, bf16[4,9,64,512]{3,2,1,0:T(8,128)(2,1)S(1)}, u32[]{:S(2)}, u32[]{:S(2)}) collective-permute-start(bf16[4,9,64,512]{3,2,1,0:T(8,128)(2,1)} %get-tuple-element.82), channel_id=1, source_target_pairs={{0,4},{4,0},{8,12},{12,8},{16,20},{20,16},{24,28},{28,24},{1,5},{5... | collective-permute-start | bytes 7077896 | tf_op jit(solution)/shard_map/ppermute | solution.py:667
  473.0 37.0 %collective-permute-start.37 = (bf16[9,64,512]{2,1,0:T(8,128)(2,1)S(1)}, bf16[9,64,512]{2,1,0:T(8,128)(2,1)S(1)}, u32[]{:S(2)}, u32[]{:S(2)}) collective-permute-start(bf16[9,64,512]{2,1,0:T(8,128)(2,1)S(1)} %get-tuple-element.146), channel_id=1, source_target_pairs={{0,1},{1,0},{2,3},{3,2},{4,5},{5,4},{6,7},{7,6},{8,9},{9,8},{10,11... | collective-permute-start | bytes 1769480 | tf_op jit(solution)/shard_map/ppermute | solution.py:663
  473.6 47.7 %collective-permute-start.39 = (bf16[9,64,512]{2,1,0:T(8,128)(2,1)S(1)}, bf16[9,64,512]{2,1,0:T(8,128)(2,1)S(1)}, u32[]{:S(2)}, u32[]{:S(2)}) collective-permute-start(bf16[9,64,512]{2,1,0:T(8,128)(2,1)S(1)} %get-tuple-element.147), channel_id=1, source_target_pairs={{0,3},{1,2},{2,1},{3,0},{4,7},{5,6},{6,5},{7,4},{8,11},{9,10},{10,... | collective-permute-start | bytes 1769480 | tf_op jit(solution)/shard_map/ppermute | solution.py:663
  484.7 37.9 %collective-permute-start.38 = (bf16[9,64,512]{2,1,0:T(8,128)(2,1)S(1)}, bf16[9,64,512]{2,1,0:T(8,128)(2,1)S(1)}, u32[]{:S(2)}, u32[]{:S(2)}) collective-permute-start(bf16[9,64,512]{2,1,0:T(8,128)(2,1)S(1)} %get-tuple-element.148), channel_id=1, source_target_pairs={{0,2},{1,3},{2,0},{3,1},{4,6},{5,7},{6,4},{7,5},{8,10},{9,11},{10,... | collective-permute-start | bytes 1769480 | tf_op jit(solution)/shard_map/ppermute | solution.py:663
  (56 other events, 897.0 us)

commit v2 on v1

--- a/solution.py
+++ b/solution.py
@@ -300,7 +300,7 @@
 BF = jnp.bfloat16
 F32 = jnp.float32
 TILE = 256
-ROWS = 64
+ROWS = 16
 ANY = pl.BlockSpec(memory_space=pl.ANY)
 SMEM = pl.BlockSpec(memory_space=pltpu.SMEM)
 LIMIT = 56 * 1024 * 1024
@@ -363,18 +363,6 @@
                     )
 
 
-def weight_copies(me, core, own, others, swapped, full, sem):
-    result = [(own, pl.ds(pl.multiple_of(me * 128, 128), 128))]
-    for k in (1, 2, 3):
-        base = jnp.bitwise_xor(me, k) * 128
-        result.append((others[k - 1], pl.ds(pl.multiple_of(base + core * 64, 64), 64)))
-        result.append((swapped[k - 1], pl.ds(pl.multiple_of(base + (1 - core) * 64, 64), 64)))
-    return [
-        pltpu.make_async_copy(part, full.at[:, rows, :], sem.at[i])
-        for i, (part, rows) in enumerate(result)
-    ]
-
-
 def demodulate(full, square_row, demod):
     chunk = 32
 
@@ -389,98 +377,177 @@
         demod[rows, :] = jnp.broadcast_to(lax.rsqrt(total + epsilon), (chunk, 128))
 
 
-def up_kernel(ids, gains, x0, x1, x2, x3, own, g1, g2, g3, s1, s2, s3, cols, rows_ref, noise,
-              raised, scaled_two, full, scaled_one, demod, copies, sem):
-    j = pl.program_id(0)
-    me, core = ids[0], ids[1]
-
-    @pl.when(j == 0)
-    def _():
-        moves = weight_copies(me, core, own, (g1, g2, g3), (s1, s2, s3), full, sem)
-        for item in moves:
+def chan_peer(me, k):
+    if k == 1:
+        return me + 1 - 2 * (me % 2)
+    return (me + 2) % 4 if k == 2 else 3 - me
+
+
+def rows_of(base, size):
+    return pl.ds(pl.multiple_of(base, size), size)
+
+
+def forward_kernel(gains, x0, x1, x2, x3, own1, g1, g2, g3, s1, s2, s3, own2, feat_grad,
+                   cols, rows_ref, noise1, noise2, order, rgb_rows,
+                   raised_out, scaled_out, conv_out, feat_out, full1_out, full2_out, grad_out,
+                   scaled_one, demod1, demod2, color,
+                   raised, scaled, full1, full2, copies, conv_tile, feat_tile, ordered,
+                   load_sem, store_sem, tile_sem, send_sem, recv_sem, swap_send, swap_recv, grad_send, grad_recv):
+    me = lax.axis_index("chan")
+    row = lax.axis_index("dp")
+    core = row % 2
+    twin = row + 1 - 2 * core
+    barrier = pltpu.get_barrier_semaphore()
+    for k in (1, 2, 3):
+        pl.semaphore_signal(barrier, inc=1, device_id={"chan": chan_peer(me, k)}, device_id_type=pl.DeviceIdType.MESH)
+    pl.semaphore_signal(barrier, inc=1, device_id={"dp": twin}, device_id_type=pl.DeviceIdType.MESH)
+    pl.semaphore_wait(barrier, 4)
+
+    mine = rows_of(me * 128 + core * 64, 64)
+    weight_moves = [
+        pltpu.make_async_remote_copy(
+            own2.at[:, rows_of(core * 64, 64), :], full2.at[:, mine, :], send_sem.at[k - 1], recv_sem.at[k - 1],
+            device_id={"chan": chan_peer(me, k)}, device_id_type=pl.DeviceIdType.MESH,
+        )
+        for k in (1, 2, 3)
+    ]
+    for item in weight_moves:
+        item.start()
+    swap_moves = []
+    for k in (1, 2, 3):
+        part = rows_of(chan_peer(me, k) * 128 + core * 64, 64)
+        swap_moves.append(
+            pltpu.make_async_remote_copy(
+                full2.at[:, part, :], full2.at[:, part, :], swap_send.at[k - 1], swap_recv.at[k - 1],
+                device_id={"dp": twin}, device_id_type=pl.DeviceIdType.MESH,
+            )
+        )
+    local2 = pltpu.make_async_copy(own2, full2.at[:, rows_of(me * 128, 128), :], load_sem.at[7])
+    local2.start()
+    loads = [pltpu.make_async_copy(own1, full1.at[:, rows_of(me * 128, 128), :], load_sem.at[0])]
+    for k, (same, other) in enumerate(((g1, s1), (g2, s2), (g3, s3))):
+        base = chan_peer(me, k + 1) * 128
+        loads.append(pltpu.make_async_copy(same, full1.at[:, rows_of(base + core * 64, 64), :], load_sem.at[1 + k]))
+        loads.append(pltpu.make_async_copy(other, full1.at[:, rows_of(base + 64 - core * 64, 64), :], load_sem.at[4 + k]))
+    for item in loads:
+        item.start()
+
+    for k, part in enumerate((x0, x1, x2, x3)):
+        base = me * 128 if k == 0 else chan_peer(me, k) * 128
+
+        @pl.loop(0, 128 // 32)
+        def _(i):
+            rows = rows_of(base + i * 32, 32)
+            style = jnp.concatenate([cols[0, rows, :]] * 8, axis=1)
+            value = (part[rows_of(i * 32, 32), :].astype(F32) * style).astype(BF)
+            scaled_one[rows, :] = value
+            for r in (0, 1):
+                for q in (0, 1):
+                    copies[2 * r + q, rows, :] = move(value, r, q)
+
+    for item in loads:
+        item.wait()
+    store1 = pltpu.make_async_copy(full1, full1_out, store_sem.at[0])
+    store1.start()
+    demodulate(full1, rows_ref[0:1, :], demod1)
+
+    @pl.loop(0, raised.shape[2] // TILE)
+    def _(j):
+        here = rows_of(j * TILE, TILE)
+        for phase, (row_phase, col_phase) in enumerate(phase_pairs):
+            total = None
+            for k, r in phase_taps[row_phase]:
+                for l, q in phase_taps[col_phase]:
+                    term = dot(full1[3 * k + l], copies[2 * r + q, :, here])
+                    total = term if total is None else total + term
+            raised[phase, :, here] = total
+            noise_row = gains[0] * noise1[phase : phase + 1, here]
+            for i in range(raised.shape[1] // ROWS):
+                rows = slice(i * ROWS, (i + 1) * ROWS)
+                pre = raised[phase, rows, here] * wide(demod1[rows, :]) + noise_row + wide(cols[3, rows, :])
+                act = pre * (0.6 * root_two + 0.4 * root_two * jnp.tanh(0.5 * pre))
+                scaled[phase, rows, here] = (act * wide(cols[1, rows, :])).astype(BF)
+
+    stores = [
+        pltpu.make_async_copy(raised, raised_out, store_sem.at[1]),
+        pltpu.make_async_copy(scaled, scaled_out, store_sem.at[2]),
+    ]
+    for item in stores:
+        item.start()
+    make_copies(scaled, copies)
+    for item, swap in zip(weight_moves, swap_moves):
+        item.wait_recv()
+        swap.start()
+    grad_moves = [
+        pltpu.make_async_remote_copy(
+            feat_grad.at[chan_peer(me, k)], grad_out.at[rows_of(me * 128, 128), :], grad_send.at[k - 1], grad_recv.at[k - 1],
+            device_id={"chan": chan_peer(me, k)}, device_id_type=pl.DeviceIdType.MESH,
+        )
+        for k in (1, 2, 3)
+    ]
+    for item in grad_moves:
+        item.start()
+    local3 = pltpu.make_async_copy(feat_grad.at[me], grad_out.at[rows_of(me * 128, 128), :], store_sem.at[4])
+    local3.start()
+    local2.wait()
+    for swap in swap_moves:
+        swap.wait_recv()
+    store2 = pltpu.make_async_copy(full2, full2_out, store_sem.at[3])
+    store2.start()
+    demodulate(full2, rows_ref[1:2, :], demod2)
+    live = gains[2]
+
+    def tile_stores(j, slot):
+        return (
+            pltpu.make_async_copy(conv_tile.at[slot], conv_out.at[:, :, rows_of(j * TILE, TILE)], tile_sem.at[0, slot]),
+            pltpu.make_async_copy(feat_tile.at[slot], feat_out.at[:, rows_of(j * 4 * TILE, 4 * TILE)], tile_sem.at[1, slot]),
+        )
+
+    @pl.loop(0, raised.shape[2] // TILE)
+    def _(j):
+        here = rows_of(j * TILE, TILE)
+        slot = j % 2
+
+        @pl.when(j >= 2)
+        def _():
+            for item in tile_stores(j - 2, slot):
+                item.wait()
+
+        for phase in range(4):
+            total = None
+            for t in range(9):
+                term = dot(full2[t], copies[copy_index(phase, t // 3 - 1, t % 3 - 1), :, here])
+                total = term if total is None else total + term
+            conv_tile[slot, phase] = total
+            noise_row = gains[1] * noise2[phase : phase + 1, here]
+            for i in range(raised.shape[1] // ROWS):
+                rows = slice(i * ROWS, (i + 1) * ROWS)
+                pre = conv_tile[slot, phase, rows, :] * wide(demod2[rows, :]) + noise_row + wide(cols[4, rows, :])
+                act = pre * (0.6 * root_two + 0.4 * root_two * jnp.tanh(0.5 * pre))
+                out = (act * live).astype(BF)
+                for half in range(TILE // 128):
+                    ordered[half, rows, phase * 128 : (phase + 1) * 128] = out[:, half * 128 : (half + 1) * 128]
+        for half in range(TILE // 128):
+            image = dot(ordered[half], order[...]).astype(BF)
+            feat_tile[slot, :, half * 512 : (half + 1) * 512] = image
+            color[:, rows_of(j * 4 * TILE + half * 512, 512)] = dot(rgb_rows[...], image)
+        for item in tile_stores(j, slot):
             item.start()
-        for k, part in enumerate((x0, x1, x2, x3)):
-            base = jnp.bitwise_xor(me, k) * 128
-
-            @pl.loop(0, 128 // 32)
-            def _(i):
-                rows = pl.ds(pl.multiple_of(base + i * 32, 32), 32)
-                here = pl.ds(pl.multiple_of(i * 32, 32), 32)
-                style = jnp.concatenate([cols[0, rows, :]] * 8, axis=1)
-                value = (part[here, :].astype(F32) * style).astype(BF)
-                scaled_one[rows, :] = value
-                for r in (0, 1):
-                    for q in (0, 1):
-                        copies[2 * r + q, rows, :] = move(value, r, q)
-
-        for item in moves:
+
+    for j in (2, 3):
+        for item in tile_stores(j, j % 2):
             item.wait()
-        demodulate(full, rows_ref[0:1, :], demod)
-
-    here = pl.ds(pl.multiple_of(j * TILE, TILE), TILE)
-    for phase, (row_phase, col_phase) in enumerate(phase_pairs):
-        total = None
-        for k, r in phase_taps[row_phase]:
-            for l, q in phase_taps[col_phase]:
-                term = dot(full[3 * k + l], copies[2 * r + q, :, here])
-                total = term if total is None else total + term
-        raised[phase] = total
-        noise_row = gains[0] * noise[phase : phase + 1, here]
-
-        @pl.loop(0, raised.shape[1] // ROWS)
-        def _(i):
-            rows = pl.ds(pl.multiple_of(i * ROWS, ROWS), ROWS)
-            pre = raised[phase, rows, :] * wide(demod[rows, :]) + noise_row + wide(cols[3, rows, :])
-            act = leaky_silu(pre)
-            scaled_two[phase, rows, :] = (act * wide(cols[1, rows, :])).astype(BF)
-
-
-def conv_kernel(ids, gains, scaled_two, own, g1, g2, g3, s1, s2, s3, cols, rows_ref, noise, order, rgb_rows,
-                convolved, f0, f1, f2, f3, color, full, demod, copies, ordered, for_rgb, sem):
-    j = pl.program_id(0)
-    me, core = ids[0], ids[1]
-
-    @pl.when(j == 0)
-    def _():
-        moves = weight_copies(me, core, own, (g1, g2, g3), (s1, s2, s3), full, sem)
-        for item in moves:
-            item.start()
-        make_copies(scaled_two, copies)
-        for item in moves:
-            item.wait()
-        demodulate(full, rows_ref[1:2, :], demod)
-
-    here = pl.ds(pl.multiple_of(j * TILE, TILE), TILE)
-    live = gains[2]
-    for phase in range(4):
-        total = None
-        for t in range(9):
-            term = dot(full[t], copies[copy_index(phase, t // 3 - 1, t % 3 - 1), :, here])
-            total = term if total is None else total + term
-        convolved[phase] = total
-        noise_row = gains[1] * noise[phase : phase + 1, here]
-
-        @pl.loop(0, convolved.shape[1] // ROWS)
-        def _(i):
-            rows = pl.ds(pl.multiple_of(i * ROWS, ROWS), ROWS)
-            pre = convolved[phase, rows, :] * wide(demod[rows, :]) + noise_row + wide(cols[4, rows, :])
-            act = leaky_silu(pre)
-            out = (act * live).astype(BF)
-            for half in range(TILE // 128):
-                ordered[half, rows, phase * 128 : (phase + 1) * 128] = out[:, half * 128 : (half + 1) * 128]
-            for_rgb[rows, :] = (act * wide(cols[2, rows, :])).astype(BF)
-
-        color[phase] = dot(rgb_rows[...], for_rgb[...])
-    for half in range(TILE // 128):
-        for k, out in enumerate((f0, f1, f2, f3)):
-            rows = pl.ds(pl.multiple_of(jnp.bitwise_xor(me, k) * 128, 128), 128)
-            out[:, half * 512 : (half + 1) * 512] = dot(ordered[half, rows, :], order[...]).astype(BF)
-
-
-def cot_kernel(ids, gains, convolved, d0, d1, d2, d3, cols, demod, noise, order, color_cot, rgb_cols,
+    for item in [store1, store2, local3] + stores:
+        item.wait()
+    for item in weight_moves + swap_moves:
+        item.wait_send()
+    for item in grad_moves:
+        item.wait()
+
+
+def cot_kernel(gains, convolved, arrived, cols, demod, noise, order, color_cot, rgb_cols,
                cot_two, sums, rgb_grad, inner, fields, for_rgb):
     j = pl.program_id(0)
-    me = ids[0]
     live = gains[2]
 
     @pl.when(j == 0)
@@ -489,11 +556,9 @@
         rgb_grad[...] = jnp.zeros_like(rgb_grad)
 
     for half in range(TILE // 128):
-        for k, part in enumerate((d0, d1, d2, d3)):
-            rows = pl.ds(pl.multiple_of(jnp.bitwise_xor(me, k) * 128, 128), 128)
-            value = dot(part[:, half * 512 : (half + 1) * 512], order[...])
-            for phase in range(4):
-                fields[phase, rows, half * 128 : (half + 1) * 128] = value[:, phase * 128 : (phase + 1) * 128]
+        value = dot(arrived[:, half * 512 : (half + 1) * 512], order[...])
+        for phase in range(4):
+            fields[phase, :, half * 128 : (half + 1) * 128] = value[:, phase * 128 : (phase + 1) * 128]
 
     here = pl.ds(pl.multiple_of(j * TILE, TILE), TILE)
     for phase in range(4):
@@ -501,14 +566,13 @@
         noise_row = gains[1] * noise_plain
         cot_here = color_cot[phase, :, here]
 
-        @pl.loop(0, convolved.shape[1] // ROWS)
-        def _(i):
-            rows = pl.ds(pl.multiple_of(i * ROWS, ROWS), ROWS)
+        for i in range(convolved.shape[1] // ROWS):
+            rows = slice(i * ROWS, (i + 1) * ROWS)
             conv = convolved[phase, rows, :]
             scale = wide(demod[rows, :])
             style = wide(cols[2, rows, :])
             pre = conv * scale + noise_row + wide(cols[4, rows, :])
-            sigma = jax.nn.sigmoid(pre)
+            sigma = 0.5 + 0.5 * jnp.tanh(0.5 * pre)
             act = root_two * (0.2 * pre + 0.8 * (pre * sigma))
             slope = root_two * (0.2 + 0.8 * sigma * (1.0 + pre * (1.0 - sigma)))
             back = dot(rgb_cols[rows, :], cot_here)
@@ -583,13 +647,12 @@
         noise_plain = noise[phase : phase + 1, here]
         noise_row = gains[0] * noise_plain
 
-        @pl.loop(0, back.shape[0] // ROWS)
-        def _(i):
-            rows = pl.ds(pl.multiple_of(i * ROWS, ROWS), ROWS)
+        for i in range(back.shape[0] // ROWS):
+            rows = slice(i * ROWS, (i + 1) * ROWS)
             conv = raised[phase, rows, :]
             scale = wide(demod[rows, :])
             pre = conv * scale + noise_row + wide(cols[3, rows, :])
-            sigma = jax.nn.sigmoid(pre)
+            sigma = 0.5 + 0.5 * jnp.tanh(0.5 * pre)
             act = root_two * (0.2 * pre + 0.8 * (pre * sigma))
             slope = root_two * (0.2 + 0.8 * sigma * (1.0 + pre * (1.0 - sigma)))
             value = back[rows, :]
@@ -647,7 +710,7 @@
                 )
 
 
-def call(kernel, grid, ins, outs, scratch, args):
+def call(kernel, grid, flops, ins, outs, scratch, args):
     return pl.pallas_call(
         kernel,
         grid=(grid,),
@@ -656,6 +719,7 @@
         out_shape=[jax.ShapeDtypeStruct(shape, dtype) for shape, dtype, _ in outs],
         scratch_shapes=scratch,
         compiler_params=pltpu.CompilerParams(vmem_limit_bytes=LIMIT),
+        cost_estimate=pl.CostEstimate(flops=flops, bytes_accessed=12 << 20, transcendentals=0),
     )(*args)
 
 
@@ -741,22 +805,17 @@
     x = [x[0]] + [quad(x[k], k) for k in (1, 2, 3)]
 
     half_one = lax.dynamic_slice_in_dim(conv_first, core * 64, 64, 1)
-    half_two = lax.dynamic_slice_in_dim(conv_second, core * 64, 64, 1)
     one_others = [quad(half_one, k) for k in (1, 2, 3)]
     one_swapped = [pair(part) for part in one_others]
-    half_two = after(half_two, one_others[2])
-    two_others = [quad(half_two, k) for k in (1, 2, 3)]
-    two_swapped = [pair(part) for part in two_others]
-    d = [pick(feat_grad, to[k], 1) for k in range(4)]
-    d = [d[0]] + [quad(after(d[k], two_others[2]), k) for k in (1, 2, 3)]
+    grad_by_image = feat_grad.transpose(1, 0, 2)
 
     noise_one = to_phases(pick(noise_first, me, 0))
     noise_two = to_phases(pick(noise_second, me, 0))
     order = phase_order()
     cot_mine = (pick(rgb_grad, me, 0) * live).astype(BF)
     color_cot = jnp.pad(to_phases(cot_mine), ((0, 0), (0, 13), (0, 0)))
-    rgb_rows = jnp.pad(rgb_all.astype(BF), ((0, 13), (0, 0)))
-    rgb_cols = rgb_rows.T
+    rgb_rows = jnp.pad((rgb_all * style_mine[2:3]).astype(BF), ((0, 13), (0, 0)))
+    rgb_cols = jnp.pad(rgb_all.astype(BF), ((0, 13), (0, 0))).T
 
     tiles = half_pix // TILE
     vec = ((channels, 128), F32, whole((channels, 128)))
@@ -767,46 +826,45 @@
     image_spec = pl.BlockSpec((local_ch, 4 * TILE), lambda j: (0, j))
     x_spec = whole((local_ch, half_pix))
 
-    raised, scaled_two, full_one, scaled_one, demod_one = call(
-        up_kernel,
-        tiles,
-        [SMEM, SMEM] + [x_spec] * 4 + [ANY] * 7 + [cols_spec, row_spec, noise_spec],
-        [
-            ((4, channels, half_pix), F32, tile_spec),
-            ((4, channels, half_pix), BF, tile_spec),
-            ((9, channels, channels), BF, full_spec),
-            ((channels, half_pix), BF, whole((channels, half_pix))),
-            vec,
+    vmem = pl.BlockSpec(memory_space=pltpu.VMEM)
+    field, wide_weight = (4, channels, half_pix), (9, channels, channels)
+    (raised, scaled_two, convolved, feat_natural, full_one, full_two, grad_arrived,
+     scaled_one, demod_one, demod_two, color) = pl.pallas_call(
+        forward_kernel,
+        in_specs=[SMEM] + [vmem] * 4 + [ANY] * 9 + [vmem] * 6,
+        out_specs=[ANY] * 7 + [vmem] * 4,
+        out_shape=[
+            jax.ShapeDtypeStruct(shape, dtype)
+            for shape, dtype in (
+                (field, F32), (field, BF), (field, F32), ((channels, pixels), BF), (wide_weight, BF),
+                (wide_weight, BF), ((channels, pixels), BF), ((channels, half_pix), BF), ((channels, 128), F32),
+                ((channels, 128), F32), ((16, pixels), F32),
+            )
         ],
-        [pltpu.VMEM((4, channels, half_pix), BF), pltpu.SemaphoreType.DMA((7,))],
-        (ids, gains, *x, conv_first, *one_others, *one_swapped, cols, squares, noise_one),
-    )
-
-    convolved, f0, f1, f2, f3, color, full_two, demod_two = call(
-        conv_kernel,
-        tiles,
-        [SMEM, SMEM, field_spec] + [ANY] * 7
-        + [cols_spec, row_spec, noise_spec, whole((512, 512)), whole((16, channels))],
-        [((4, channels, half_pix), F32, tile_spec)]
-        + [((local_ch, pixels), BF, image_spec)] * 4
-        + [
-            ((4, 16, half_pix), F32, pl.BlockSpec((4, 16, TILE), lambda j: (0, 0, j))),
-            ((9, channels, channels), BF, full_spec),
-            vec,
-        ],
-        [
+        scratch_shapes=[
+            pltpu.VMEM(field, F32),
+            pltpu.VMEM(field, BF),
+            pltpu.VMEM(wide_weight, BF),
+            pltpu.VMEM(wide_weight, BF),
             pltpu.VMEM((16, channels, half_pix), BF),
+            pltpu.VMEM((2, 4, channels, TILE), F32),
+            pltpu.VMEM((2, channels, 4 * TILE), BF),
             pltpu.VMEM((TILE // 128, channels, 512), BF),
-            pltpu.VMEM((channels, TILE), BF),
-            pltpu.SemaphoreType.DMA((7,)),
-        ],
-        (ids, gains, scaled_two, conv_second, *two_others, *two_swapped, cols, squares, noise_two, order, rgb_rows),
-    )
+            pltpu.SemaphoreType.DMA((8,)),
+            pltpu.SemaphoreType.DMA((5,)),
+            pltpu.SemaphoreType.DMA((2, 2)),
+        ]
+        + [pltpu.SemaphoreType.DMA((3,))] * 6,
+        compiler_params=pltpu.CompilerParams(vmem_limit_bytes=LIMIT, collective_id=0, has_side_effects=True),
+        cost_estimate=pl.CostEstimate(flops=int(50e9), bytes_accessed=12 << 20, transcendentals=0),
+    )(gains, *x, conv_first, *one_others, *one_swapped, conv_second, grad_by_image, cols, squares,
+      noise_one, noise_two, order, rgb_rows)
 
     cot_two, sums_two, rgb_part, inner_two = call(
         cot_kernel,
         tiles,
-        [SMEM, SMEM, tile_spec] + [image_spec] * 4
+        int(12e9),
+        [SMEM, tile_spec, pl.BlockSpec((channels, 4 * TILE), lambda j: (0, j))]
         + [cols_spec, whole((channels, 128)), noise_spec, whole((512, 512)), whole((4, 16, half_pix)),
            whole((channels, 16))],
         [
@@ -816,7 +874,7 @@
             vec,
         ],
         [pltpu.VMEM((4, channels, TILE), F32), pltpu.VMEM((channels, TILE), BF)],
-        (ids, gains, convolved, *d, cols, demod_two, noise_two, order.T, color_cot, rgb_cols),
+        (gains, convolved, grad_arrived, cols, demod_two, noise_two, order.T, color_cot, rgb_cols),
     )
 
     grad_spec = pl.BlockSpec((4, 1, 64, channels), lambda t: (0, t, 0, 0))
@@ -824,6 +882,7 @@
     keep_two, send_two = call(
         second_grad_kernel,
         9,
+        int(22e9),
         [SMEM, field_spec, field_spec, full_spec, whole((channels, 128)), row_spec],
         [grad_shape, grad_shape],
         [pltpu.VMEM((16, channels, half_pix), BF), pltpu.VMEM((channels, channels), F32)],
@@ -834,6 +893,7 @@
     cot_one, sums_one, inner_one = call(
         second_back_kernel,
         tiles,
+        int(35e9),
         [SMEM, SMEM, field_spec, full_spec, tile_spec, cols_spec, whole((channels, 128)), noise_spec],
         [
             ((4, channels, half_pix), BF, tile_spec),
@@ -851,6 +911,7 @@
     keep_one, send_one, b0, b1, b2, b3, sums_zero = call(
         first_kernel,
         9,
+        int(15e9),
         [SMEM, field_spec, whole((channels, half_pix)), full_spec, whole((channels, 128)), cols_spec, row_spec]
         + [x_spec] * 4,
         [grad_shape, grad_shape] + [((local_ch, half_pix), BF, x_spec)] * 4 + [vec],
@@ -863,13 +924,14 @@
     )
     grad_one = reduce_grad(keep_one, send_one, me, depth)
 
-    feat_out = [f0] + [quad(after(part, d[3]), k + 1) for k, part in enumerate((f1, f2, f3))]
+    feat_out = [lax.dynamic_slice_in_dim(feat_natural, to[k] * local_ch, local_ch, 0) for k in range(4)]
+    feat_out = [feat_out[0]] + [quad(feat_out[k], k) for k in (1, 2, 3)]
     feat_out = natural(feat_out, me).transpose(1, 0, 2)
     back = [b0] + [quad(part, k + 1) for k, part in enumerate((b1, b2, b3))]
     feat_in_grad = natural(back, me).transpose(1, 0, 2).astype(F32)
 
     lift_matrix = upsample_matrix(HALF)
-    color = color[:, :3].reshape(2, 2, 3, HALF, HALF).transpose(2, 3, 0, 4, 1).reshape(3, pixels)
+    color = color[:3]
     shard_pix = pixels // 4
     color = color.reshape(3, 4, shard_pix)
     color = [pick(color, to[k], 1) for k in range(4)]

time: 579 us -> 504 us (0.87)
  Pallas kernels: 239 us -> 193 us
  local copies, waits for them, and re-layouts: 83.9 us -> 54.7 us
    pallas_call x6 -> x4, Pallas kernels: 239 us -> 114 us  [call(): pl.pallas_call(kernel, grid=(grid,), in_specs=ins, out_specs=[spec for _,...]
    pallas_call x0 -> x1, Pallas kernels: none -> 78.8 us  [image_body(): pl.pallas_call(forward_kernel, in_specs=[SMEM] + [vmem] * 4 + [ANY] * 9 +...]
    dynamic_slice x4 -> x3, local copies, waits for them, and re-layouts: 20.3 us -> 3.16 us  [pick(): return lax.dynamic_index_in_dim(value, index, axis, keepdims=False)]
    ppermute x12, starting transfers between devices: 22.6 us -> 33.2 us  [along(): return lax.ppermute(value, 'dp', [(i, i ^ 2 * k) for i in range(8)])]
    ppermute x36 -> x30, starting transfers between devices: 44.6 us -> 37.6 us  [quad(): return lax.ppermute(value, 'chan', [(i, i ^ k) for i in range(4)])]
    ppermute x12, waiting for transfers between devices: 19.9 us -> 13.1 us  [along(): return lax.ppermute(value, 'dp', [(i, i ^ 2 * k) for i in range(8)])]
    ppermute x36 -> x30, waiting for transfers between devices: 98.4 us -> 105 us  [quad(): return lax.ppermute(value, 'chan', [(i, i ^ k) for i in range(4)])]
    unnamed x70 -> x73, local copies, waits for them, and re-layouts: 12.3 us -> 12 us
  transfers between devices with their start and end apart: 58 -> 49, of which waited for: 19 -> 17; matrix products, arithmetic and copies ran while one was open for 19% -> 15% of each run, Pallas kernels for 21% -> 7%
where the time goes in v2:
time: 504 us; the launch traced here: 495 us
  Pallas kernels  193 us (38%)
  waiting for transfers between devices  118 us (23%)
  starting transfers between devices  71.5 us (14%)
  local copies, waits for them, and re-layouts  54.7 us (11%)
  other arithmetic  25.6 us (5%)
  blocking collectives  23.9 us (5%)
    pallas_call x4, Pallas kernels, call(): pl.pallas_call(kernel, grid=(grid,), in_specs=ins, out_specs=[spec for _,...  114 us
    ppermute x30, waiting for transfers between devices, quad(): return lax.ppermute(value, 'chan', [(i, i ^ k) for i in range(4)])  105 us
    pallas_call x1, Pallas kernels, image_body(): pl.pallas_call(forward_kernel, in_specs=[SMEM] + [vmem] * 4 + [ANY] * 9 +...  78.8 us
    ppermute x30, starting transfers between devices, quad(): return lax.ppermute(value, 'chan', [(i, i ^ k) for i in range(4)])  37.6 us
    ppermute x12, starting transfers between devices, along(): return lax.ppermute(value, 'dp', [(i, i ^ 2 * k) for i in range(8)])  33.2 us
    all_gather x1, blocking collectives, image_body(): gathered = lax.all_gather(gathered, 'dp')  14.5 us
    ppermute x12, waiting for transfers between devices, along(): return lax.ppermute(value, 'dp', [(i, i ^ 2 * k) for i in range(8)])  13.1 us
    unnamed x73, local copies, waits for them, and re-layouts  12 us
  transfers between devices with their start and end apart: 49, of which 17 were waited for; matrix products, arithmetic and copies ran while one was open for 15% of the time, Pallas kernels for 7%

profile of v2, /device:TPU:0, one launch (start us, length us, event | category | flops | bytes accessed | tf_op | source)
XLA Modules:
  0.0 494.7 jit_solution(8373769176028688215)
XLA Ops:
  31.4 6.5 %copy.196 = bf16[128,4,4096]{2,0,1:T(8,128)(2,1)} copy(bf16[128,4,4096]{2,1,0:T(4,128)(2,1)} %param.30) | data formatting | bytes 8388608 | tf_op args[14]
  37.9 4.6 convert_element_type.224
  53.2 12.0 %collective-permute-done.5.g3 = bf16[9,64,512]{2,1,0:T(8,128)(2,1)S(1)} collective-permute-done((bf16[9,64,512]{2,1,0:T(8,128)(2,1)S(1)}, bf16[9,64,512]{2,1,0:T(8,128)(2,1)S(1)}, u32[]{:S(2)}, u32[]{:S(2)}) %collective-permute-start.5) | collective-permute-done | bytes 589856 | tf_op jit(solution)/shard_map/ppermute | solution.py:727
  69.5 6.9 %collective-permute-done.2.x3 = bf16[128,1024]{1,0:T(8,128)(2,1)S(1)} collective-permute-done((bf16[128,1024]{1,0:T(8,128)(2,1)}, bf16[128,1024]{1,0:T(8,128)(2,1)S(1)}, u32[]{:S(2)}, u32[]{:S(2)}) %collective-permute-start.2) | collective-permute-done | bytes 262176 | tf_op jit(solution)/shard_map/ppermute | solution.py:727
  78.0 78.8 %shard_map.255 = (f32[4,512,1024]{2,1,0:T(8,128)}, bf16[4,512,1024]{2,1,0:T(8,128)(2,1)}, f32[4,512,1024]{2,1,0:T(8,128)}, bf16[512,4096]{1,0:T(8,128)(2,1)}, bf...) custom-call(f32[3]{0:T(128)} %pad_maximum_fusion.15.gains, ...), custom_call_target="tpu_custom_call" | custom-call | flops 49999998976 | bytes 12582912 | tf_op jit(solution)/shard_map/pallas_call | solution.py:832
  156.8 16.6 %shard_map.256 = (bf16[4,512,1024]{2,1,0:T(8,128)(2,1)}, f32[4,512,128]{2,1,0:T(8,128)}, f32[16,512]{1,0:T(8,128)}, f32[512,128]{1,0:T(8,128)}) custom-call(f32[3]{0:T(128)} %pad_maximum_fusion.15.gains, f32[4,512,1024]{2,1,0:T(8,128)} %get-tuple-element.42.convolved, bf16[512,4096]{1,0:T(8,128)(2,1)} %get-tuple-element.43.arrived, ...), custom_call_target="tpu_custom_call" | custom-call | flops 12000000000 | bytes 12582912 | tf_op jit(solution)/shard_map/pallas_call | solution.py:714
  175.6 39.9 %shard_map.257 = (bf16[4,512,1024]{2,1,0:T(8,128)(2,1)}, f32[4,512,128]{2,1,0:T(8,128)}, f32[512,128]{1,0:T(8,128)}) custom-call(s32[2]{0:T(128)} %pad_add_fusion.ids, f32[3]{0:T(128)} %pad_maximum_fusion.15.gains, bf16[4,512,1024]{2,1,0:T(8,128)(2,1)} %get-tuple-element.45.cot_two, bf16[9,512,512]{2,1,0:T(8,128)(2,1)} %get-tuple-element.46.full, ...), custom_call_target="tpu_custom_call" | custom-call | flops 35000000512 | bytes 12582912 | tf_op jit(solution)/shard_map/pallas_call | solution.py:714
  217.6 24.3 %shard_map.258 = (bf16[4,9,64,512]{3,2,1,0:T(8,128)(2,1)}, bf16[4,9,64,512]{3,2,1,0:T(8,128)(2,1)}, bf16[128,1024]{1,0:T(8,128)(2,1)}, bf16[128,1024]{1,0:T(8,12...) custom-call(s32[2]{0:T(128)} %pad_add_fusion.ids, ...), custom_call_target="tpu_custom_call" | custom-call | flops 15000000512 | bytes 12582912 | tf_op jit(solution)/shard_map/pallas_call | solution.py:714
  248.2 33.6 %shard_map.259 = (bf16[4,9,64,512]{3,2,1,0:T(8,128)(2,1)}, bf16[4,9,64,512]{3,2,1,0:T(8,128)(2,1)}) custom-call(s32[2]{0:T(128)} %pad_add_fusion.ids, bf16[4,512,1024]{2,1,0:T(8,128)(2,1)} %get-tuple-element.45.cot_two, bf16[4,512,1024]{2,1,0:T(8,128)(2,1)} %get-tuple-element.64.scaled_two, bf16[9,512,512]{2,1,0:T(8,128)(2,1)} %get-tuple-element.46.full, ...), custom_call_target="tpu_custom_call" | custom-call | flops 22000001024 | bytes 12582912 | tf_op jit(solution)/shard_map/pallas_call | solution.py:714
  283.3 3.9 dynamic-slice_bitcast_fusion
  291.2 14.5 %all-gather.1 = f32[8,57,128]{2,1,0:T(8,128)S(1)} all-gather(f32[1,57,128]{2,1,0:T(8,128)S(1)} %fusion.27), channel_id=2, replica_groups=mesh['dp'=8,'chan'=4] {'dp'}, dimensions={0}, use_global_device_ids=true | all-gather | bytes 262656 | tf_op jit(solution)/shard_map/all_gather | solution.py:982
  309.3 9.4 %psum.7 = f32[2]{0:T(128)} all-reduce(f32[2]{0:T(128)S(1)} %get-tuple-element.157), channel_id=1, replica_groups=mesh['dp'=8,'chan'=4] {'chan'}, use_global_device_ids=true, to_apply=%region_9.10 | all-reduce | flops 2 | bytes 16 | tf_op jit(solution)/shard_map/psum | solution.py:988
  324.0 4.1 collective-permute-done.24
  345.6 17.5 %collective-permute-done.12 = bf16[128,4096]{1,0:T(8,128)(2,1)S(1)} collective-permute-done((bf16[128,4096]{1,0:T(8,128)(2,1)}, bf16[128,4096]{1,0:T(8,128)(2,1)S(1)}, u32[]{:S(2)}, u32[]{:S(2)}) %collective-permute-start.12) | collective-permute-done | bytes 1048608 | tf_op jit(solution)/shard_map/ppermute | solution.py:727
  363.1 23.0 %collective-permute-done.14 = bf16[128,4096]{1,0:T(8,128)(2,1)S(1)} collective-permute-done((bf16[128,4096]{1,0:T(8,128)(2,1)}, bf16[128,4096]{1,0:T(8,128)(2,1)S(1)}, u32[]{:S(2)}, u32[]{:S(2)}) %collective-permute-start.14) | collective-permute-done | bytes 1048608 | tf_op jit(solution)/shard_map/ppermute | solution.py:727
  397.5 9.3 %collective-permute-done.39 = bf16[9,64,512]{2,1,0:T(8,128)(2,1)S(1)} collective-permute-done((bf16[9,64,512]{2,1,0:T(8,128)(2,1)S(1)}, bf16[9,64,512]{2,1,0:T(8,128)(2,1)S(1)}, u32[]{:S(2)}, u32[]{:S(2)}) %collective-permute-start.39) | collective-permute-done | bytes 589856 | tf_op jit(solution)/shard_map/ppermute | solution.py:727
  409.7 10.6 %collective-permute-done.40 = bf16[9,64,512]{2,1,0:T(8,128)(2,1)S(1)} collective-permute-done((bf16[9,64,512]{2,1,0:T(8,128)(2,1)S(1)}, bf16[9,64,512]{2,1,0:T(8,128)(2,1)S(1)}, u32[]{:S(2)}, u32[]{:S(2)}) %collective-permute-start.40) | collective-permute-done | bytes 589856 | tf_op jit(solution)/shard_map/ppermute | solution.py:727
  424.7 7.5 %collective-permute-done.28 = bf16[9,64,512]{2,1,0:T(8,128)(2,1)S(1)} collective-permute-done((bf16[9,64,512]{2,1,0:T(8,128)(2,1)S(1)}, bf16[9,64,512]{2,1,0:T(8,128)(2,1)S(1)}, u32[]{:S(2)}, u32[]{:S(2)}) %collective-permute-start.28) | collective-permute-done | bytes 589856 | tf_op jit(solution)/shard_map/ppermute | solution.py:727
  432.1 3.3 collective-permute-start.44
  435.5 8.3 %collective-permute-done.29 = bf16[9,64,512]{2,1,0:T(8,128)(2,1)S(1)} collective-permute-done((bf16[9,64,512]{2,1,0:T(8,128)(2,1)S(1)}, bf16[9,64,512]{2,1,0:T(8,128)(2,1)S(1)}, u32[]{:S(2)}, u32[]{:S(2)}) %collective-permute-start.29) | collective-permute-done | bytes 589856 | tf_op jit(solution)/shard_map/ppermute | solution.py:727
  456.2 3.5 collective-permute-done.32
  459.8 12.2 %collective-permute-start.34 = (bf16[9,16,512]{2,1,0:T(8,128)(2,1)S(1)}, bf16[9,16,512]{2,1,0:T(8,128)(2,1)S(1)}, u32[]{:S(2)}, u32[]{:S(2)}) collective-permute-start(bf16[9,16,512]{2,1,0:T(8,128)(2,1)S(1)} %fusion.17), channel_id=1, source_target_pairs={{0,8},{4,12},{8,0},{12,4},{16,24},{20,28},{24,16},{28,20},{1,9},{5... | collective-permute-start | bytes 442376 | tf_op jit(solution)/shard_map/ppermute | solution.py:1023
  476.8 7.1 %collective-permute-done.35 = bf16[9,16,512]{2,1,0:T(8,128)(2,1)S(1)} collective-permute-done((bf16[9,16,512]{2,1,0:T(8,128)(2,1)S(1)}, bf16[9,16,512]{2,1,0:T(8,128)(2,1)S(1)}, u32[]{:S(2)}, u32[]{:S(2)}) %collective-permute-start.35) | collective-permute-done | bytes 147488 | tf_op jit(solution)/shard_map/ppermute | solution.py:1023
  485.3 5.3 %copy.195 = bf16[4,128,4096]{2,0,1:T(4,128)(2,1)} copy(bf16[4,128,4096]{2,1,0:T(8,128)(2,1)S(1)} %bitcast.254) | data formatting | bytes 8388608 | tf_op jit(solution)/shard_map/reshape | solution.py:743
  (285 shorter events, 129.4 us)
Async XLA Ops:
  1.9 50.7 %collective-permute-start.3 = (bf16[9,64,512]{2,1,0:T(8,128)(2,1)S(1)}, bf16[9,64,512]{2,1,0:T(8,128)(2,1)}, u32[]{:S(2)}, u32[]{:S(2)}) collective-permute-start(bf16[9,64,512]{2,1,0:T(8,128)(2,1)S(1)} %constant_dynamic-slice_fusion.14), channel_id=1, source_target_pairs={{0,1},{1,0},{2,3},{3,2},{4,5},{5,4},{6,7},{7,6},{8,9},{9,8},{10,11... | collective-permute-start | bytes 1769480 | tf_op jit(solution)/shard_map/ppermute | solution.py:727
  4.9 47.8 %collective-permute-start.4 = (bf16[9,64,512]{2,1,0:T(8,128)(2,1)S(1)}, bf16[9,64,512]{2,1,0:T(8,128)(2,1)}, u32[]{:S(2)}, u32[]{:S(2)}) collective-permute-start(bf16[9,64,512]{2,1,0:T(8,128)(2,1)S(1)} %constant_dynamic-slice_fusion.14), channel_id=1, source_target_pairs={{0,2},{1,3},{2,0},{3,1},{4,6},{5,7},{6,4},{7,5},{8,10},{9,11},{10,... | collective-permute-start | bytes 1769480 | tf_op jit(solution)/shard_map/ppermute | solution.py:727
  9.1 39.0 %collective-permute-start.10 = (f32[8,128]{1,0:T(8,128)S(1)}, f32[8,128]{1,0:T(8,128)}, u32[]{:S(2)}, u32[]{:S(2)}) collective-permute-start(f32[8,128]{1,0:T(8,128)S(1)} %get-tuple-element.173), channel_id=1, source_target_pairs={{0,2},{1,3},{2,0},{3,1},{4,6},{5,7},{6,4},{7,5},{8,10},{9,11},{10,... | collective-permute-start | bytes 12296 | tf_op jit(solution)/shard_map/ppermute | solution.py:727
  9.6 38.5 %collective-permute-start.11 = (f32[8,128]{1,0:T(8,128)S(1)}, f32[8,128]{1,0:T(8,128)}, u32[]{:S(2)}, u32[]{:S(2)}) collective-permute-start(f32[8,128]{1,0:T(8,128)S(1)} %get-tuple-element.174), channel_id=1, source_target_pairs={{0,3},{1,2},{2,1},{3,0},{4,7},{5,6},{6,5},{7,4},{8,11},{9,10},{10,... | collective-permute-start | bytes 12296 | tf_op jit(solution)/shard_map/ppermute | solution.py:727
  11.1 39.0 %collective-permute-start.9 = (f32[8,128]{1,0:T(8,128)S(1)}, f32[8,128]{1,0:T(8,128)}, u32[]{:S(2)}, u32[]{:S(2)}) collective-permute-start(f32[8,128]{1,0:T(8,128)S(1)} %get-tuple-element.172), channel_id=1, source_target_pairs={{0,1},{1,0},{2,3},{3,2},{4,5},{5,4},{6,7},{7,6},{8,9},{9,8},{10,11... | collective-permute-start | bytes 12296 | tf_op jit(solution)/shard_map/ppermute | solution.py:727
  244.6 42.8 %collective-permute-start.21 = (f32[10,128]{1,0:T(8,128)S(1)}, f32[10,128]{1,0:T(8,128)S(1)}, u32[]{:S(2)}, u32[]{:S(2)}) collective-permute-start(f32[10,128]{1,0:T(8,128)S(1)} %bitcast.313), channel_id=1, source_target_pairs={{0,1},{1,0},{2,3},{3,2},{4,5},{5,4},{6,7},{7,6},{8,9},{9,8},{10,11... | collective-permute-start | bytes 15368 | tf_op jit(solution)/shard_map/ppermute | solution.py:727
  245.3 43.7 %collective-permute-start.22 = (f32[10,128]{1,0:T(8,128)S(1)}, f32[10,128]{1,0:T(8,128)S(1)}, u32[]{:S(2)}, u32[]{:S(2)}) collective-permute-start(f32[10,128]{1,0:T(8,128)S(1)} %bitcast.312), channel_id=1, source_target_pairs={{0,2},{1,3},{2,0},{3,1},{4,6},{5,7},{6,4},{7,5},{8,10},{9,11},{10,... | collective-permute-start | bytes 15368 | tf_op jit(solution)/shard_map/ppermute | solution.py:727
  245.3 43.7 %collective-permute-start.23 = (f32[10,128]{1,0:T(8,128)S(1)}, f32[10,128]{1,0:T(8,128)S(1)}, u32[]{:S(2)}, u32[]{:S(2)}) collective-permute-start(f32[10,128]{1,0:T(8,128)S(1)} %bitcast.311), channel_id=1, source_target_pairs={{0,3},{1,2},{2,1},{3,0},{4,7},{5,6},{6,5},{7,4},{8,11},{9,10},{10,... | collective-permute-start | bytes 15368 | tf_op jit(solution)/shard_map/ppermute | solution.py:727
  281.8 105.1 %collective-permute-start.38 = (bf16[4,9,64,512]{3,2,1,0:T(8,128)(2,1)}, bf16[4,9,64,512]{3,2,1,0:T(8,128)(2,1)}, u32[]{:S(2)}, u32[]{:S(2)}) collective-permute-start(bf16[4,9,64,512]{3,2,1,0:T(8,128)(2,1)} %get-tuple-element.66), channel_id=1, source_target_pairs={{0,4},{4,0},{8,12},{12,8},{16,20},{20,16},{24,28},{28,24},{1,5},{5... | collective-permute-start | bytes 7077896 | tf_op jit(solution)/shard_map/ppermute | solution.py:731
  281.8 55.2 %collective-permute-start.18 = (bf16[128,1024]{1,0:T(8,128)(2,1)}, bf16[128,1024]{1,0:T(8,128)(2,1)}, u32[]{:S(2)}, u32[]{:S(2)}) collective-permute-start(bf16[128,1024]{1,0:T(8,128)(2,1)} %get-tuple-element.54), channel_id=1, source_target_pairs={{0,1},{1,0},{2,3},{3,2},{4,5},{5,4},{6,7},{7,6},{8,9},{9,8},{10,11... | collective-permute-start | bytes 786440 | tf_op jit(solution)/shard_map/ppermute | solution.py:727
  287.4 32.5 %collective-permute-start.15 = (f32[3,1024]{1,0:T(4,128)S(1)}, f32[3,1024]{1,0:T(4,128)S(1)}, u32[]{:S(2)}, u32[]{:S(2)}) collective-permute-start(f32[3,1024]{1,0:T(4,128)S(1)} %bitcast.306), channel_id=1, source_target_pairs={{0,1},{1,0},{2,3},{3,2},{4,5},{5,4},{6,7},{7,6},{8,9},{9,8},{10,11... | collective-permute-start | bytes 36872 | tf_op jit(solution)/shard_map/ppermute | solution.py:727
  288.9 32.4 %collective-permute-start.16 = (f32[3,1024]{1,0:T(4,128)S(1)}, f32[3,1024]{1,0:T(4,128)S(1)}, u32[]{:S(2)}, u32[]{:S(2)}) collective-permute-start(f32[3,1024]{1,0:T(4,128)S(1)} %bitcast.305), channel_id=1, source_target_pairs={{0,2},{1,3},{2,0},{3,1},{4,6},{5,7},{6,4},{7,5},{8,10},{9,11},{10,... | collective-permute-start | bytes 36872 | tf_op jit(solution)/shard_map/ppermute | solution.py:727
  289.0 32.9 %collective-permute-start.17 = (f32[3,1024]{1,0:T(4,128)S(1)}, f32[3,1024]{1,0:T(4,128)S(1)}, u32[]{:S(2)}, u32[]{:S(2)}) collective-permute-start(f32[3,1024]{1,0:T(4,128)S(1)} %bitcast.304), channel_id=1, source_target_pairs={{0,3},{1,2},{2,1},{3,0},{4,7},{5,6},{6,5},{7,4},{8,11},{9,10},{10,... | collective-permute-start | bytes 36872 | tf_op jit(solution)/shard_map/ppermute | solution.py:727
  336.9 57.1 %collective-permute-start.27 = (bf16[4,9,64,512]{3,2,1,0:T(8,128)(2,1)}, bf16[4,9,64,512]{3,2,1,0:T(8,128)(2,1)S(1)}, u32[]{:S(2)}, u32[]{:S(2)}) collective-permute-start(bf16[4,9,64,512]{3,2,1,0:T(8,128)(2,1)} %get-tuple-element.63), channel_id=1, source_target_pairs={{0,4},{4,0},{8,12},{12,8},{16,20},{20,16},{24,28},{28,24},{1,5},{5... | collective-permute-start | bytes 7077896 | tf_op jit(solution)/shard_map/ppermute | solution.py:731
  336.9 26.2 %collective-permute-start.12 = (bf16[128,4096]{1,0:T(8,128)(2,1)}, bf16[128,4096]{1,0:T(8,128)(2,1)S(1)}, u32[]{:S(2)}, u32[]{:S(2)}) collective-permute-start(bf16[128,4096]{1,0:T(8,128)(2,1)} %get-tuple-element.124), channel_id=1, source_target_pairs={{0,1},{1,0},{2,3},{3,2},{4,5},{5,4},{6,7},{7,6},{8,9},{9,8},{10,11... | collective-permute-start | bytes 3145736 | tf_op jit(solution)/shard_map/ppermute | solution.py:727
  337.5 25.7 %collective-permute-start.13 = (bf16[128,4096]{1,0:T(8,128)(2,1)}, bf16[128,4096]{1,0:T(8,128)(2,1)S(1)}, u32[]{:S(2)}, u32[]{:S(2)}) collective-permute-start(bf16[128,4096]{1,0:T(8,128)(2,1)} %get-tuple-element.123), channel_id=1, source_target_pairs={{0,2},{1,3},{2,0},{3,1},{4,6},{5,7},{6,4},{7,5},{8,10},{9,11},{10,... | collective-permute-start | bytes 3145736 | tf_op jit(solution)/shard_map/ppermute | solution.py:727
  338.5 47.6 %collective-permute-start.14 = (bf16[128,4096]{1,0:T(8,128)(2,1)}, bf16[128,4096]{1,0:T(8,128)(2,1)S(1)}, u32[]{:S(2)}, u32[]{:S(2)}) collective-permute-start(bf16[128,4096]{1,0:T(8,128)(2,1)} %get-tuple-element.122), channel_id=1, source_target_pairs={{0,3},{1,2},{2,1},{3,0},{4,7},{5,6},{6,5},{7,4},{8,11},{9,10},{10,... | collective-permute-start | bytes 3145736 | tf_op jit(solution)/shard_map/ppermute | solution.py:727
  391.4 28.9 %collective-permute-start.40 = (bf16[9,64,512]{2,1,0:T(8,128)(2,1)S(1)}, bf16[9,64,512]{2,1,0:T(8,128)(2,1)S(1)}, u32[]{:S(2)}, u32[]{:S(2)}) collective-permute-start(bf16[9,64,512]{2,1,0:T(8,128)(2,1)S(1)} %get-tuple-element.127), channel_id=1, source_target_pairs={{0,2},{1,3},{2,0},{3,1},{4,6},{5,7},{6,4},{7,5},{8,10},{9,11},{10,... | collective-permute-start | bytes 1769480 | tf_op jit(solution)/shard_map/ppermute | solution.py:727
  392.9 27.4 %collective-permute-start.41 = (bf16[9,64,512]{2,1,0:T(8,128)(2,1)S(1)}, bf16[9,64,512]{2,1,0:T(8,128)(2,1)S(1)}, u32[]{:S(2)}, u32[]{:S(2)}) collective-permute-start(bf16[9,64,512]{2,1,0:T(8,128)(2,1)S(1)} %get-tuple-element.126), channel_id=1, source_target_pairs={{0,3},{1,2},{2,1},{3,0},{4,7},{5,6},{6,5},{7,4},{8,11},{9,10},{10,... | collective-permute-start | bytes 1769480 | tf_op jit(solution)/shard_map/ppermute | solution.py:727
  395.2 37.0 %collective-permute-start.28 = (bf16[9,64,512]{2,1,0:T(8,128)(2,1)S(1)}, bf16[9,64,512]{2,1,0:T(8,128)(2,1)S(1)}, u32[]{:S(2)}, u32[]{:S(2)}) collective-permute-start(bf16[9,64,512]{2,1,0:T(8,128)(2,1)S(1)} %get-tuple-element.128), channel_id=1, source_target_pairs={{0,1},{1,0},{2,3},{3,2},{4,5},{5,4},{6,7},{7,6},{8,9},{9,8},{10,11... | collective-permute-start | bytes 1769480 | tf_op jit(solution)/shard_map/ppermute | solution.py:727
  396.1 47.6 %collective-permute-start.29 = (bf16[9,64,512]{2,1,0:T(8,128)(2,1)S(1)}, bf16[9,64,512]{2,1,0:T(8,128)(2,1)S(1)}, u32[]{:S(2)}, u32[]{:S(2)}) collective-permute-start(bf16[9,64,512]{2,1,0:T(8,128)(2,1)S(1)} %get-tuple-element.130), channel_id=1, source_target_pairs={{0,2},{1,3},{2,0},{3,1},{4,6},{5,7},{6,4},{7,5},{8,10},{9,11},{10,... | collective-permute-start | bytes 1769480 | tf_op jit(solution)/shard_map/ppermute | solution.py:727
  406.8 36.9 %collective-permute-start.30 = (bf16[9,64,512]{2,1,0:T(8,128)(2,1)S(1)}, bf16[9,64,512]{2,1,0:T(8,128)(2,1)S(1)}, u32[]{:S(2)}, u32[]{:S(2)}) collective-permute-start(bf16[9,64,512]{2,1,0:T(8,128)(2,1)S(1)} %get-tuple-element.129), channel_id=1, source_target_pairs={{0,3},{1,2},{2,1},{3,0},{4,7},{5,6},{6,5},{7,4},{8,11},{9,10},{10,... | collective-permute-start | bytes 1769480 | tf_op jit(solution)/shard_map/ppermute | solution.py:727
  420.7 27.3 %collective-permute-start.42 = (bf16[9,16,512]{2,1,0:T(8,128)(2,1)S(1)}, bf16[9,16,512]{2,1,0:T(8,128)(2,1)S(1)}, u32[]{:S(2)}, u32[]{:S(2)}) collective-permute-start(bf16[9,16,512]{2,1,0:T(8,128)(2,1)S(1)} %get-tuple-element.139), channel_id=1, source_target_pairs={{0,8},{4,12},{8,0},{12,4},{16,24},{20,28},{24,16},{28,20},{1,9},{5... | collective-permute-start | bytes 442376 | tf_op jit(solution)/shard_map/ppermute | solution.py:1023
  422.3 26.3 %collective-permute-start.43 = (bf16[9,16,512]{2,1,0:T(8,128)(2,1)S(1)}, bf16[9,16,512]{2,1,0:T(8,128)(2,1)S(1)}, u32[]{:S(2)}, u32[]{:S(2)}) collective-permute-start(bf16[9,16,512]{2,1,0:T(8,128)(2,1)S(1)} %get-tuple-element.141), channel_id=1, source_target_pairs={{0,16},{4,20},{8,24},{12,28},{16,0},{20,4},{24,8},{28,12},{1,17},{... | collective-permute-start | bytes 442376 | tf_op jit(solution)/shard_map/ppermute | solution.py:1023
  (49 other events, 724.2 us)
